TPU v7x, 128 devices: a whole 4x4x4 slice. The times are simulated.
128 devices in a mesh: cls: 4 (over z_lo, core), dom: 32 (over x, z_hi, y).
Axes of the slice: x: 4, y: 4, z: 4 (z_hi: 2, z_lo: 2; z = z_hi * 2 + z_lo), core: 2. Of those that a mesh axis runs over, the one named last changes fastest.
Arguments:
- particles: bfloat16 [12288, 128, 128], P('dom'), may hold values from -600 to 600
- references: bfloat16 [128, 128, 128], P('cls', 'dom'), may hold values from -0.6 to 0.6
- ctf_table: float32 [64, 128], replicated, may hold values from 0.1 to 1
- noise_inv: float32 [128], replicated, may hold values from 0.05 to 0.5
- groups: int32 [12288], P('dom'), may hold values from 0 to 63
- prior_rot: int32 [12288], P('dom'), may hold values from 0 to 15
Outputs:
- new_refs: float32 [128, 128, 128], P('cls', 'dom')
- loglik: float32 [12288], P('dom')
All inputs are finite; a program needn't handle non-finite values.
Results may differ from a plain program's by a relative error of at most 0.0026.
Values may be sent and summed in bfloat16 or wider, within the bound.
No kernel may reach another device: no remote copies, remote signals or barrier semaphores. Data moves between devices by JAX's collectives and lax.ppermute only.
A program may use at most 192 MiB of HBM per device.

v0:
```python
import jax
import jax.numpy as jnp
from jax import lax
from jax.sharding import PartitionSpec as P

ROTS = 16


PRIOR_WEIGHT = 0.02
TIKHONOV = 1.0


def local(particles, references, ctf_table, noise_inv, groups, prior_rot):
    count = particles.shape[0]
    cycles = particles.shape[1]
    angles = particles.shape[2]
    classes_here = references.shape[0]
    group_count = ctf_table.shape[0]
    step = angles // ROTS
    choose = (groups[:, None] == jnp.arange(group_count, dtype=jnp.int32)[None, :]).astype(
        jnp.float32
    )
    ctf_part = jnp.dot(choose, ctf_table, precision=lax.Precision.HIGHEST)
    cycle_weight = ctf_part * noise_inv[None, :]
    weighted = (particles.astype(jnp.float32) * cycle_weight[:, :, None]).astype(jnp.bfloat16)
    ctf_power = ctf_table * ctf_table * noise_inv[None, :]

    def accumulate(piece):
        width = piece.shape[1]
        rotated = jnp.stack([jnp.roll(piece, turn * step, axis=2) for turn in range(ROTS)])
        rotated = rotated.reshape(ROTS * classes_here, width * angles)
        window = weighted.reshape(count, width * angles)
        corr_sum = lax.dot_general(
            window, rotated, (((1,), (1,)), ((), ())), preferred_element_type=jnp.float32
        )
        piece_float = piece.astype(jnp.float32)
        power = jnp.sum(piece_float * piece_float, axis=2)
        norm_sum = jnp.dot(ctf_power, power.T, precision=lax.Precision.HIGHEST)
        return (corr_sum, norm_sum)

    corr, norm_table = accumulate(lax.all_gather(references, "dom", axis=1, tiled=True))
    corr = corr.reshape(count, ROTS, classes_here)
    norm_part = jnp.dot(choose, norm_table, precision=lax.Precision.HIGHEST)
    turns = jnp.arange(ROTS, dtype=jnp.int32)
    offset = (turns[None, :] - prior_rot[:, None]) % ROTS
    distance = jnp.minimum(offset, ROTS - offset).astype(jnp.float32)
    prior = -PRIOR_WEIGHT * distance * distance
    score = corr - 0.5 * norm_part[:, None, :] + prior[:, :, None]
    local_peak = jnp.max(score, axis=(1, 2))
    peak = lax.pmax(local_peak, "cls")
    expo = jnp.exp(score - peak[:, None, None])
    total = lax.psum(jnp.sum(expo, axis=(1, 2)), "cls")
    loglik = peak + jnp.log(total)
    resp = (expo / total[:, None, None]).astype(jnp.bfloat16)
    flat = weighted.reshape(count, cycles * angles)
    sums = lax.dot_general(
        resp.reshape(count, ROTS * classes_here),
        flat,
        (((0,), (0,)), ((), ())),
        preferred_element_type=jnp.float32,
    )
    sums = sums.reshape(ROTS, classes_here, cycles, angles)
    numer = jnp.zeros((classes_here, cycles, angles), jnp.float32)
    for turn in range(ROTS):
        numer = numer + jnp.roll(sums[turn], -turn * step, axis=2)
    class_weight = jnp.sum(resp.astype(jnp.float32), axis=1)
    ctf_rows = jnp.dot(choose, ctf_power, precision=lax.Precision.HIGHEST)
    denom = lax.dot_general(
        class_weight, ctf_rows, (((0,), (0,)), ((), ())), precision=lax.Precision.HIGHEST
    )
    share = cycles // lax.axis_size("dom")
    position = lax.axis_index("dom") * share
    numer_here = lax.psum_scatter(numer, "dom", scatter_dimension=1, tiled=True)
    denom_all = lax.psum(denom, "dom")
    denom_here = lax.dynamic_slice_in_dim(denom_all, position, share, 1)
    new_refs = numer_here / (denom_here[:, :, None] + TIKHONOV)
    return (new_refs, loglik)


def solution(mesh):
    in_specs = (P("dom", None, None), P("cls", "dom", None), P(), P(), P("dom"), P("dom"))
    out_specs = (P("cls", "dom", None), P("dom"))
    return jax.shard_map(local, mesh=mesh, in_specs=in_specs, out_specs=out_specs, check_vma=False)
```

profile of v0, /device:TPU:0, one launch (start us, length us, event | category | flops | bytes accessed | tf_op | source)
XLA Modules:
  0.0 510.6 jit_solution(10358706571009006917)
XLA Ops:
  10.5 11.5 %multiply_convert_fusion = bf16[384,128,128]{2,1,0:T(8,128)(2,1)} fusion(bf16[384,128,128]{2,1,0:T(8,128)(2,1)} %param.6, f32[384,128]{1,0:T(8,128)S(1)} %convolution_multiply_fusion), kind=kLoop, calls=%fused_computation | loop fusion | flops 18874368 | bytes 25362432 | tf_op jit(solution)/shard_map/convert_element_type | solution.py:25
  21.9 59.4 %all-gather.2.cloned.1.call-done = bf16[32,128,128]{2,0,1:T(8,128)(2,1)} async-done(((bf16[32,4,128]{2,0,1:T(8,128)(2,1)}), bf16[32,128,128]{2,0,1:T(8,128)(2,1)}) %all-gather.2.cloned.1.call-update) | async-done | bytes 1048592 | tf_op jit(solution)/shard_map/all_gather | solution.py:41
  114.7 33.0 %fusion.73 = (f32[384]{0:T(512)S(1)}, f32[384,16,32]{0,2,1:T(8,128)S(1)}) fusion(f32[384,16]{0,1:T(8,128)S(1)} %multiply_multiply_fusion, f32[384,32]{0,1:T(8,128)S(1)} %convolution_multiply_fusion.1, bf16[16,32,128,128]{3,1,2,0:T(8,128)(2,1)} %fusion.43, bf16[384,128,128]{2,1,0:T(8,128)(2,1)} %multiply_convert_fusion), kind=kOutput, calls=%fused_computation.117 | convolution fusion | flops 6443040256 | bytes 30221824 | tf_op jit(solution)/shard_map/dot_general | solution.py:33
  147.7 5.7 %pmax.7 = f32[384]{0:T(512)S(1)} all-reduce(f32[384]{0:T(512)S(1)} %get-tuple-element.54), channel_id=1, replica_groups=mesh['cls'=4,'dom'=32] {'cls'}, use_global_device_ids=true, to_apply=%region_2.3 | all-reduce | flops 384 | bytes 3072 | tf_op jit(solution)/shard_map/pmax | solution.py:50
  153.5 6.0 %psum.14 = f32[384]{0:T(512)S(1)} all-reduce(f32[384]{0:T(512)S(1)} %fusion.44), channel_id=1, replica_groups=mesh['cls'=4,'dom'=32] {'cls'}, use_global_device_ids=true, to_apply=%region_4.5 | all-reduce | flops 384 | bytes 3072 | tf_op jit(solution)/shard_map/psum | solution.py:52
  159.7 27.1 %fusion = f32[512,16384]{1,0:T(8,128)} fusion(bf16[384,512]{0,1:T(8,128)(2,1)S(1)} %bitcast.214, bf16[48,8,128,128]{3,2,1,0:T(8,128)(2,1)} %bitcast.184), kind=kOutput, calls=%fused_computation.1 | convolution fusion | flops 6442450944 | bytes 46530560 | tf_op jit(solution)/shard_map/dot_general | solution.py:56
  186.8 21.4 %slice_bitcast_fusion = (f32[4,8,128,128]{3,1,2,0:T(8,128)}, f32[4,8,128,128]{3,1,2,0:T(8,128)}, f32[4,8,128,128]{3,1,2,0:T(8,128)}, f32[4,8,128,128]{3,1,2,0:T(...) fusion(f32[512,16384]{1,0:T(8,128)} %fusion), kind=kLoop, calls=%fused_computation.22 | loop fusion | bytes 67108864
  221.1 2.9 copy.52
  225.0 2.6 copy.54
  228.6 2.6 copy.56
  232.2 2.6 copy.58
  239.3 2.6 copy.64
  253.6 2.6 copy.72
  259.7 2.8 copy.47
  265.1 2.6 copy.51
  272.7 2.6 copy.57
  277.8 2.6 copy.63
  280.4 2.6 copy.65
  283.0 2.8 copy.67
  285.7 2.6 copy.69
  293.3 2.6 copy.75
  295.9 21.0 %fusion.19 = f32[32,128,128]{2,0,1:T(8,128)} fusion(f32[4,128,8,128]{3,2,1,0:T(8,128)S(1)} %get-tuple-element.21, f32[32,128,8]{2,0,1:T(8,128)} %copy.47, f32[32,128,120]{2,0,1:T(8,128)S(1)} %copy.46, f32[32,128,16]{2,0,1:T(8,128)} %copy.49, f32[32,128,112]{2,0,1:T(8,128)S(1)} %copy.48, f32[32,128,24]{2,0,1:T(8,128)} %copy.51, f32[32,128,104]{2,0,1:T(8,128)} %copy.50, ...), kind=kLoop, calls=%fused_computation.21 | loop fusion | flops 15728640 | bytes 35651584 | tf_op jit(solution)/shard_map/add | solution.py:65
  318.5 180.0 %psum.15 = f32[32,128]{0,1:T(8,128)S(1)} all-reduce(f32[32,128]{0,1:T(8,128)S(1)} %fusion.74), channel_id=1, replica_groups=mesh['cls'=4,'dom'=32] {'dom'}, use_global_device_ids=true, to_apply=%region_7.8 | all-reduce | flops 4096 | bytes 32768 | tf_op jit(solution)/shard_map/psum | solution.py:74
  499.1 2.6 reduce-scatter.2.cloned.1.call-done
  (133 shorter events, 91.2 us)
Async XLA Ops:
  7.2 74.1 %all-gather.2.cloned.1.call-start = ((), (), s32[]{:S(2)}) async-start(), calls=%async_computation.1 | async-start | bytes 1081344 | tf_op jit(solution)/shard_map/all_gather | solution.py:41
  8.6 493.1 %reduce-scatter.2.cloned.1.call-start = ((), (), s32[]{:S(2)}) async-start(), calls=%async_computation.2 | async-start | bytes 2162688 | tf_op jit(solution)/shard_map/reduce_scatter | solution.py:73
  10.4 72.8 %copy-start.13 = (f32[64,128]{1,0:T(8,128)S(1)}, f32[64,128]{1,0:T(8,128)}, u32[]{:S(2)}) copy-start(f32[64,128]{1,0:T(8,128)} %param.8) | copy-start | bytes 98308
  10.4 72.8 %copy-start.17 = (f32[128]{0:T(128)S(1)}, f32[128]{0:T(128)}, u32[]{:S(2)}) copy-start(f32[128]{0:T(128)} %param.9) | copy-start | bytes 1540
  10.5 73.0 %copy-start.15 = (s32[384]{0:T(512)S(1)}, s32[384]{0:T(512)}, u32[]{:S(2)}) copy-start(s32[384]{0:T(512)} %param.10) | copy-start | bytes 4612
  81.3 2.5 copy-start
  215.0 1.6 copy-start.12
  217.6 2.6 copy-start.11
  221.1 2.9 copy-start.10
  225.0 2.6 copy-start.9
  228.6 2.6 copy-start.8
  232.2 2.6 copy-start.7
  235.8 2.6 copy-start.6
  239.3 2.6 copy-start.5
  243.0 2.5 copy-start.4
  246.5 2.6 copy-start.3
  250.1 2.5 copy-start.2
  253.6 2.6 copy-start.1
  316.9 0.8 copy-start.14
  316.9 0.8 copy-start.16
  316.9 0.7 copy-start.18
Sparse Core Ops, SparseCore 0:
  11.6 69.7 all-gather.1
  317.1 184.5 reduce-scatter.1
where the time goes:
time: 520 us; the launch traced here: 511 us
  blocking collectives  192 us (37%)
  local copies, waits for them, and re-layouts  119 us (23%)
  matrix products  62.4 us (12%)
  waiting for transfers between devices  62 us (12%)
  other arithmetic  60.9 us (12%)
  between operations  15 us (3%)
    psum x1, blocking collectives, local(): denom_all = lax.psum(denom, 'dom')  180 us
    unnamed x87, local copies, waits for them, and re-layouts  104 us
    all_gather x1, waiting for transfers between devices, local(): lax.all_gather(references, 'dom', axis=1, tiled=True)  59.4 us
    dot_general x1, matrix products, accumulate(): lax.dot_general(window, rotated, (((1,), (1,)), ((), ())), preferred_elem...  33 us
    dot_general x1, matrix products, local(): lax.dot_general(resp.reshape(count, ROTS * classes_here), flat, (((0,), (...  27.1 us
    unnamed x14, other arithmetic  22.5 us
    add x1, other arithmetic, local(): numer = numer + jnp.roll(sums[turn], -turn * step, axis=2)  21 us
    convert_element_type x1, other arithmetic, local(): (particles.astype(jnp.float32) * cycle_weight[:, :, None]).astype(jnp.bfl...  11.5 us
  transfers between devices with their start and end apart: 2, of which 2 were waited for; matrix products, arithmetic and copies ran while one was open for 3% of the time, Pallas kernels for 0%

commit v1 on v0

v1 whole, which is shorter than its diff:
```python
import jax
import jax.numpy as jnp
from jax import lax
from jax.experimental import pallas as pl
from jax.experimental.pallas import tpu as pltpu
from jax.sharding import PartitionSpec as P

ROTS = 16
PRIOR_WEIGHT = 0.02
TIKHONOV = 1.0
F32 = jnp.float32
BF16 = jnp.bfloat16
NX, NZ, NY = 4, 2, 4
VMEM = pl.BlockSpec(memory_space=pltpu.VMEM)
MIB = 2**20


def params(mib):
    return pltpu.CompilerParams(vmem_limit_bytes=mib * MIB)


def cost(flops, nbytes):
    return pl.CostEstimate(flops=flops, bytes_accessed=nbytes, transcendentals=0)


def coords(i):
    return i // (NZ * NY), (i // NY) % NZ, i % NY


def shift(dx, dz, dy):
    pairs = []
    for i in range(NX * NZ * NY):
        x, z, y = coords(i)
        pairs.append((i, ((x + dx) % NX) * NZ * NY + ((z + dz) % NZ) * NY + (y + dy) % NY))
    return pairs


def send(value, dx, dz, dy):
    return lax.ppermute(value, "dom", shift(dx, dz, dy))


def split2(value):
    high = value.astype(BF16)
    low = (value - high.astype(F32)).astype(BF16)
    return high, low


def setup_kernel(groups_ref, ctf_ref, noise_ref, weight_ref, power_ref):
    group_count, cycles = ctf_ref.shape
    count = groups_ref.shape[1]
    choose = (
        lax.broadcasted_iota(jnp.int32, (group_count, count), 0) == groups_ref[...]
    ).astype(F32)
    pick = lambda table: lax.dot_general(
        choose, table, (((0,), (0,)), ((), ())), precision=lax.Precision.HIGHEST,
        preferred_element_type=F32,
    )
    ctf = ctf_ref[...]
    noise = noise_ref[...]
    weight_ref[...] = pick(ctf) * noise
    high, low = split2(pick(ctf * ctf * noise))
    power_ref[:, :cycles] = high
    power_ref[:, cycles:] = low


def setup(groups, ctf_table, noise_inv):
    count = groups.shape[0]
    cycles = ctf_table.shape[1]
    return pl.pallas_call(
        setup_kernel,
        out_shape=(
            jax.ShapeDtypeStruct((count, cycles), F32),
            jax.ShapeDtypeStruct((count, 2 * cycles), BF16),
        ),
        in_specs=[VMEM] * 3,
        out_specs=(VMEM, VMEM),
        compiler_params=params(16),
        name="setup",
    )(groups.reshape(1, count), ctf_table, noise_inv.reshape(1, cycles))


def weigh_kernel(particles_ref, weight_ref, out_ref, wide):
    rows, cycles, _ = particles_ref.shape
    pitch = cycles + 1
    start = pl.multiple_of(pl.program_id(0) * rows, 16)
    weight = weight_ref[...]
    for n in range(rows):
        wide[pl.ds(n * pitch, cycles), :] = particles_ref[n].astype(F32)
    for q in range(cycles):
        image = wide[pl.ds(q, rows, stride=pitch), :]
        out_ref[q, pl.ds(start, rows), :] = (image * weight[:, q : q + 1]).astype(BF16)


def weigh(particles, weight, part, parts):
    count, cycles, angles = particles.shape
    here = count // parts
    rows = 48
    steps = here // rows
    return pl.pallas_call(
        weigh_kernel,
        out_shape=pltpu.VMEM((cycles, here, angles), BF16),
        grid=(steps,),
        in_specs=[
            pl.BlockSpec((rows, cycles, angles), lambda i: (part * steps + i, 0, 0)),
            pl.BlockSpec((rows, cycles), lambda i: (part * steps + i, 0)),
        ],
        out_specs=VMEM,
        scratch_shapes=[pltpu.VMEM((rows * (cycles + 1) + 8, angles), F32)],
        compiler_params=params(16),
        cost_estimate=cost(0, here * cycles * angles * 16),
        name="weigh",
    )(particles, weight)


def cycle_of(dx, j):
    dom = lax.axis_index("dom")
    x, z, y = dom // (NZ * NY), (dom // NY) % NZ, dom % NY
    dy, dz, i = j // (4 * NZ), (j // 4) % NZ, j % 4
    return ((x + dx) % NX) * (4 * NZ * NY) + ((z + dz) % NZ) * (4 * NY) + ((y + dy) % NY) * 4 + i


def correlate_steps(shifts, block_refs, image_refs, turned, total, power):
    classes, angles = block_refs[0].shape[1:]
    lane = lax.broadcasted_iota(jnp.int32, power.shape, 1)
    slot = 0
    for dx, block_ref in zip(shifts, block_refs):
        for j in range(0, block_ref.shape[0], 2):
            sides = []
            for i in range(2):
                piece = block_ref[j + i]
                cycle = cycle_of(dx, j + i)
                for turn in range(ROTS):
                    turned[slot % 4, turn * classes : (turn + 1) * classes, i * angles : (i + 1) * angles] = (
                        pltpu.roll(piece, 8 * turn, 1) if turn else piece
                    )
                wide = piece.astype(F32)
                power = jnp.where(lane == cycle, jnp.sum(wide * wide, axis=1, keepdims=True), power)
                sides.append(jnp.concatenate([ref[cycle] for ref in image_refs], axis=0))
            part = lax.dot_general(
                jnp.concatenate(sides, axis=1), turned[slot % 4], (((1,), (1,)), ((), ())),
                preferred_element_type=F32,
            )
            total = part if total is None else total + part
            slot += 1
    return total, power


def correlate(shifts, blocks, images, before):
    cycles = images[0].shape[0]
    angles = images[0].shape[2]
    count = sum(image.shape[1] for image in images)
    classes = blocks[0].shape[1]
    wide = ROTS * classes
    nb, ni = len(blocks), len(images)

    def kernel(*refs):
        block_refs, image_refs = refs[:nb], refs[nb : nb + ni]
        rest = refs[nb + ni :]
        if before is not None:
            total, power = rest[0][...], rest[1][...]
            rest = rest[2:]
        else:
            total, power = None, jnp.zeros((classes, cycles), F32)
        total_ref, power_ref, turned = rest
        total, power = correlate_steps(shifts, block_refs, image_refs, turned, total, power)
        total_ref[...] = total
        power_ref[...] = power

    extra = [] if before is None else list(before)
    return pl.pallas_call(
        kernel,
        out_shape=(pltpu.VMEM((count, wide), F32), pltpu.VMEM((classes, cycles), F32)),
        in_specs=[VMEM] * (nb + ni + len(extra)),
        out_specs=(VMEM, VMEM),
        scratch_shapes=[pltpu.VMEM((4, wide, 2 * angles), BF16)],
        compiler_params=params(24),
        cost_estimate=cost(2 * count * wide * 32 * nb * angles, 0),
        name="correlate",
    )(*blocks, *images, *extra)


def score(shifts, blocks, images, before, power_pair, prior_rot):
    cycles = images[0].shape[0]
    angles = images[0].shape[2]
    count = sum(image.shape[1] for image in images)
    classes = blocks[0].shape[1]
    wide = ROTS * classes
    nb, ni = len(blocks), len(images)

    def kernel(*refs):
        block_refs, image_refs = refs[:nb], refs[nb : nb + ni]
        total_ref, cycle_ref, pair_ref, prior_ref, expo_ref, stats_ref, turned = refs[nb + ni :]
        total, power = correlate_steps(
            shifts, block_refs, image_refs, turned, total_ref[...], cycle_ref[...]
        )
        high, low = split2(-0.5 * power)
        both = jnp.concatenate([high, high], axis=1)
        low_both = jnp.concatenate([low, low], axis=1)
        pair = pair_ref[...]
        norm = lax.dot_general(pair, both, (((1,), (1,)), ((), ())), preferred_element_type=F32)
        norm = norm + lax.dot_general(
            pair, low_both, (((1,), (1,)), ((), ())), preferred_element_type=F32
        )
        total = total + jnp.concatenate([norm] * ROTS, axis=1)
        hot = (
            lax.broadcasted_iota(jnp.int32, (2 * ROTS, count), 0) % ROTS == prior_ref[...]
        ).astype(BF16)
        row = lax.broadcasted_iota(jnp.int32, (2 * ROTS, wide), 0)
        turn = lax.broadcasted_iota(jnp.int32, (2 * ROTS, wide), 1) // classes
        offset = (turn - row + 2 * ROTS) % ROTS
        distance = jnp.minimum(offset, ROTS - offset).astype(F32)
        prior = -PRIOR_WEIGHT * distance * distance
        high, low = split2(prior)
        table = jnp.where(row < ROTS, high.astype(F32), low.astype(F32)).astype(BF16)
        total = total + lax.dot_general(
            hot, table, (((0,), (0,)), ((), ())), preferred_element_type=F32
        )
        peak = jnp.max(total, axis=1, keepdims=True)
        expo = jnp.exp(total - peak)
        expo_ref[...] = expo
        mass = jnp.sum(expo, axis=1, keepdims=True)
        lane = lax.broadcasted_iota(jnp.int32, (count, 128), 1)
        stats = jnp.transpose(jnp.where(lane < 64, peak, mass))
        stats_ref[0:8] = stats[0:8]
        stats_ref[8:16] = stats[64:72]

    return pl.pallas_call(
        kernel,
        out_shape=(pltpu.VMEM((count, wide), F32), jax.ShapeDtypeStruct((16, count), F32)),
        in_specs=[VMEM] * (nb + ni + 4),
        out_specs=(VMEM, VMEM),
        scratch_shapes=[pltpu.VMEM((4, wide, 2 * angles), BF16)],
        compiler_params=params(24),
        cost_estimate=cost(2 * count * wide * 32 * nb * angles, 0),
        name="score",
    )(*blocks, *images, *before, power_pair, prior_rot.reshape(1, count))


def turn_over_kernel(expo_ref, out_ref):
    out_ref[...] = jnp.transpose(expo_ref[...])


def turn_over(expo):
    count, wide = expo.shape
    return pl.pallas_call(
        turn_over_kernel,
        out_shape=pltpu.VMEM((wide, count), F32),
        in_specs=[VMEM],
        out_specs=VMEM,
        compiler_params=params(16),
        cost_estimate=cost(0, 4 * count * wide),
        name="turn_over",
    )(expo)


def share_kernel(expo_ref, own_ref, a_ref, b_ref, c_ref, pair_ref, resp_ref, loglik_ref, denom_ref):
    refs = (own_ref, a_ref, b_ref, c_ref)
    peaks = [ref[0:8] for ref in refs]
    peak = jnp.maximum(jnp.maximum(peaks[0], peaks[1]), jnp.maximum(peaks[2], peaks[3]))
    scales = [jnp.exp(value - peak) for value in peaks]
    total = sum(scale * ref[8:16] for scale, ref in zip(scales, refs))
    loglik_ref[...] = peak + jnp.log(total)
    factor = (scales[0] / total)[0:1]
    resp = (expo_ref[...] * factor).astype(BF16)
    resp_ref[...] = resp
    classes, cycles = denom_ref.shape
    rows = jnp.dot(resp, pair_ref[...], preferred_element_type=F32)
    rows = rows[:, :cycles] + rows[:, cycles:]
    denom = rows[:classes]
    for turn in range(1, ROTS):
        denom = denom + rows[turn * classes : (turn + 1) * classes]
    denom_ref[...] = denom


def share(expo, own, others, power_pair, classes):
    wide, count = expo.shape
    cycles = power_pair.shape[1] // 2
    return pl.pallas_call(
        share_kernel,
        out_shape=(
            pltpu.VMEM((wide, count), BF16),
            jax.ShapeDtypeStruct((8, count), F32),
            pltpu.VMEM((classes, cycles), F32),
        ),
        in_specs=[VMEM] * 6,
        out_specs=(VMEM, VMEM, VMEM),
        compiler_params=params(24),
        name="share",
    )(expo, own, *others, power_pair)


def pack_denom(denom):
    lane = lax.broadcasted_iota(jnp.int32, denom.shape, 1)
    high, low = split2(denom)
    packed = jnp.where(lane < 32, high.astype(F32), pltpu.roll(low.astype(F32), 32, 1))
    return jnp.where(lane < 64, packed, 0.0)


def join_denom(packed):
    lane = lax.broadcasted_iota(jnp.int32, packed.shape, 1)
    return jnp.where(lane < 32, packed + pltpu.roll(packed, 96, 1), 0.0)


def gather_sums(dx, resp, images, denom, dtype):
    classes, cycles = denom.shape
    angles = images[0].shape[2]
    wide, count = resp.shape
    length = 4 * NZ * NY
    ni = len(images)

    def kernel(*refs):
        resp_ref, image_refs = refs[0], refs[1 : 1 + ni]
        denom_ref, out_ref = refs[1 + ni :]
        for j in range(0, length, 2):
            side = jnp.concatenate(
                [
                    jnp.concatenate([ref[cycle_of(dx, j + i)] for ref in image_refs], axis=0)
                    for i in range(2)
                ],
                axis=1,
            )
            sums = jnp.dot(resp_ref[...], side, preferred_element_type=F32)
            for i in range(2):
                total = None
                for turn in range(ROTS):
                    piece = sums[turn * classes : (turn + 1) * classes, i * angles : (i + 1) * angles]
                    if turn:
                        piece = pltpu.roll(piece, angles - 8 * turn, 1)
                    total = piece if total is None else total + piece
                out_ref[j + i] = total.astype(dtype)
        x = lax.axis_index("dom") // (NZ * NY)
        offset = ((x + dx) % NX) * length
        mine = pltpu.roll(denom_ref[...], (cycles - offset) % cycles, 1)
        lane = lax.broadcasted_iota(jnp.int32, mine.shape, 1)
        if dtype == BF16:
            out_ref[length] = pack_denom(mine).astype(BF16)
        else:
            out_ref[length] = jnp.where(lane < length, mine, 0.0)

    return pl.pallas_call(
        kernel,
        out_shape=jax.ShapeDtypeStruct((length + 1, classes, angles), dtype),
        in_specs=[VMEM] * (ni + 2),
        out_specs=VMEM,
        compiler_params=params(24),
        cost_estimate=cost(2 * count * wide * length * angles, 0),
        name="gather_sums",
    )(resp, *images, denom)


def add_parts(own, others, ways):
    rows, classes, angles = own.shape
    length = (rows - 1) // ways

    def kernel(own_ref, *refs):
        others_ref, outs = refs[: len(others)], refs[len(others) :]
        total = own_ref[rows - 1]
        for ref in others_ref:
            total = total + ref[rows - 1].astype(F32)
        denom = join_denom(total)
        packed = pack_denom(denom).astype(BF16)
        for way in range(ways):
            for j in range(length):
                total = own_ref[way * length + j]
                for ref in others_ref:
                    total = total + ref[way * length + j].astype(F32)
                outs[way][j] = total.astype(outs[way].dtype)
            outs[way][length] = packed if way else denom

    shape = (length + 1, classes, angles)
    return pl.pallas_call(
        kernel,
        out_shape=tuple(
            jax.ShapeDtypeStruct(shape, BF16 if way else F32) for way in range(ways)
        ),
        in_specs=[VMEM] * (1 + len(others)),
        out_specs=(VMEM,) * ways,
        compiler_params=params(16),
        name="add_parts",
    )(own, *others)


def finish(own, other):
    rows, classes, angles = own.shape

    def kernel(own_ref, other_ref, out_ref):
        dom = lax.axis_index("dom")
        offset = ((dom // NY) % NZ) * (4 * NY) + (dom % NY) * 4
        denom = join_denom(own_ref[rows - 1] + other_ref[rows - 1].astype(F32))
        denom = pltpu.roll(denom, (angles - offset) % angles, 1) + TIKHONOV
        for i in range(rows - 1):
            numer = own_ref[i] + other_ref[i].astype(F32)
            out_ref[:, i, :] = numer / denom[:, i : i + 1]

    return pl.pallas_call(
        kernel,
        out_shape=jax.ShapeDtypeStruct((classes, rows - 1, angles), F32),
        in_specs=[VMEM, VMEM],
        out_specs=VMEM,
        compiler_params=params(16),
        name="finish",
    )(own, other)


def local(particles, references, ctf_table, noise_inv, groups, prior_rot):
    classes = references.shape[0]
    piece = jnp.transpose(references, (1, 0, 2))
    piece = jnp.concatenate([piece, send(piece, 0, 1, 0)], axis=0)
    piece = jnp.concatenate([piece] + [send(piece, 0, 0, -d) for d in (1, 2, 3)], axis=0)
    blocks = [piece] + [send(piece, -d, 0, 0) for d in (1, 2, 3)]

    weight, power_pair = setup(groups, ctf_table, noise_inv)
    parts = 4
    images = [weigh(particles, weight, part, parts) for part in range(parts)]

    before = correlate((0,), blocks[:1], images, None)
    before = correlate((1, 3), [blocks[1], blocks[3]], images, before)
    expo, stats = score((2,), [blocks[2]], images, before, power_pair, prior_rot)
    others = [lax.ppermute(stats, "cls", [(i, i ^ j) for i in range(4)]) for j in (1, 2, 3)]
    turned = turn_over(expo)
    resp, loglik, denom = share(turned, stats, others, power_pair, classes)

    arrived = []
    for d in (2, 1, 3):
        arrived.append(send(gather_sums(d, resp, images, denom, BF16), d, 0, 0))
    own = gather_sums(0, resp, images, denom, F32)
    pieces = add_parts(own, arrived, NY)
    arrived = [send(pieces[d], 0, 0, d) for d in (1, 2, 3)]
    pieces = add_parts(pieces[0], arrived, NZ)
    new_refs = finish(pieces[0], send(pieces[1], 0, 1, 0))
    return (new_refs, loglik[0])


def solution(mesh):
    in_specs = (P("dom", None, None), P("cls", "dom", None), P(), P(), P("dom"), P("dom"))
    out_specs = (P("cls", "dom", None), P("dom"))
    return jax.shard_map(local, mesh=mesh, in_specs=in_specs, out_specs=out_specs, check_vma=False)
```

time: 520 us -> 92.8 us (0.18); the launches traced: 511 us -> 92.4 us
  blocking collectives: 192 us -> 0 us
  local copies, waits for them, and re-layouts: 119 us -> 8.85 us
  matrix products: 62.4 us -> 0 us
  other arithmetic: 60.9 us -> 0.01 us
  waiting for transfers between devices: 62 us -> 24.6 us
  Pallas kernels: 0 us -> 29.7 us
  starting transfers between devices: 0.08 us -> 28.4 us
  between operations: 15 us -> 0.83 us
    psum x2 -> x0, blocking collectives: 186 us -> none  [the longest x1 180 us: local(): denom_all = lax.psum(denom, 'dom')]
    unnamed x87 -> x13, local copies, waits for them, and re-layouts: 104 us -> 7.55 us
    dot_general x7 -> x0, matrix products: 62.4 us -> none  [the longest x1 33 us: accumulate(): lax.dot_general(window, rotated, (((1,), (1,)), ((), ())), preferred_elem...]
    all_gather x1 -> x0, waiting for transfers between devices: 59.4 us -> none  [local(): lax.all_gather(references, 'dom', axis=1, tiled=True)]
    pallas_call x0 -> x17, Pallas kernels: none -> 29.7 us  [the longest x4 10.4 us: gather_sums(): pl.pallas_call(kernel, out_shape=jax.ShapeDtypeStruct((length + 1, classe...]
    ppermute x0 -> x17, starting transfers between devices: none -> 28.4 us  [the longest x14 26.5 us: send(): return lax.ppermute(value, 'dom', shift(dx, dz, dy))]
    ppermute x0 -> x17, waiting for transfers between devices: none -> 24.6 us  [the longest x14 21.8 us: send(): return lax.ppermute(value, 'dom', shift(dx, dz, dy))]
    unnamed x14 -> x0, other arithmetic: 22.5 us -> none
  transfers between devices with their start and end apart: 2 -> 17, of which waited for: 2 -> 12; matrix products, arithmetic and copies ran while one was open for 3% -> 2% of each run, Pallas kernels for 0% -> 19%
where the time goes in v1:
time: 92.8 us; the launch traced here: 92.4 us
  Pallas kernels  29.7 us (32%)
  starting transfers between devices  28.4 us (31%)
  waiting for transfers between devices  24.6 us (27%)
  local copies, waits for them, and re-layouts  8.85 us (10%)
    ppermute x14, starting transfers between devices, send(): return lax.ppermute(value, 'dom', shift(dx, dz, dy))  26.5 us
    ppermute x14, waiting for transfers between devices, send(): return lax.ppermute(value, 'dom', shift(dx, dz, dy))  21.8 us
    pallas_call x4, Pallas kernels, gather_sums(): pl.pallas_call(kernel, out_shape=jax.ShapeDtypeStruct((length + 1, classe...  10.4 us
    pallas_call x4, Pallas kernels, weigh(): pl.pallas_call(weigh_kernel, out_shape=pltpu.VMEM((cycles, here, angles),...  9.03 us
    unnamed x13, local copies, waits for them, and re-layouts  7.55 us
    pallas_call x2, Pallas kernels, correlate(): pl.pallas_call(kernel, out_shape=(pltpu.VMEM((count, wide), F32), pltpu.V...  5.48 us
    ppermute x3, waiting for transfers between devices, local(): lax.ppermute(stats, 'cls', [(i, i ^ j) for i in range(4)])  2.76 us
    pallas_call x1, Pallas kernels, score(): pl.pallas_call(kernel, out_shape=(pltpu.VMEM((count, wide), F32), jax.Sha...  2.42 us
  transfers between devices with their start and end apart: 17, of which 12 were waited for; matrix products, arithmetic and copies ran while one was open for 2% of the time, Pallas kernels for 19%

profile of v1, /device:TPU:0, one launch (start us, length us, event | category | flops | bytes accessed | tf_op | source)
XLA Modules:
  0.0 92.4 jit_solution(1658703454640688543)
XLA Ops:
  1.4 4.0 %collective-permute-start = (bf16[4,32,128]{2,1,0:T(8,128)(2,1)S(1)}, bf16[4,32,128]{2,1,0:T(8,128)(2,1)S(1)}, u32[]{:S(2)}, u32[]{:S(2)}) collective-permute-start(bf16[4,32,128]{2,1,0:T(8,128)(2,1)S(1)} %bitcast.7), channel_id=1, source_target_pairs={{0,4},{1,5},{2,6},{3,7},{4,0},{5,1},{6,2},{7,3},{8,12},{9,13},{10,... | collective-permute-start | bytes 98312 | tf_op jit(solution)/shard_map/ppermute | solution.py:39
  7.3 3.1 %collective-permute-start.1 = (bf16[8,32,128]{2,1,0:T(8,128)(2,1)S(1)}, bf16[8,32,128]{2,1,0:T(8,128)(2,1)S(1)}, u32[]{:S(2)}, u32[]{:S(2)}) collective-permute-start(bf16[8,32,128]{2,1,0:T(8,128)(2,1)S(1)} %pad_maximum_fusion), channel_id=1, source_target_pairs={{0,3},{1,0},{2,1},{3,2},{4,7},{5,4},{6,5},{7,6},{8,11},{9,8},{10,9... | collective-permute-start | bytes 196616 | tf_op jit(solution)/shard_map/ppermute | solution.py:39
  12.3 3.9 %collective-permute-done.2 = bf16[8,32,128]{2,1,0:T(8,128)(2,1)S(1)} collective-permute-done((bf16[8,32,128]{2,1,0:T(8,128)(2,1)S(1)}, bf16[8,32,128]{2,1,0:T(8,128)(2,1)S(1)}, u32[]{:S(2)}, u32[]{:S(2)}) %collective-permute-start.2) | collective-permute-done | bytes 65568 | tf_op jit(solution)/shard_map/ppermute | solution.py:39
  16.8 2.8 %collective-permute-start.5 = (bf16[32,32,128]{2,1,0:T(8,128)(2,1)S(1)}, bf16[32,32,128]{2,1,0:T(8,128)(2,1)S(1)}, u32[]{:S(2)}, u32[]{:S(2)}) collective-permute-start(bf16[32,32,128]{2,1,0:T(8,128)(2,1)S(1)} %constant_dynamic-update-slice_fusion.refs_0_), channel_id=1, source_target_pairs={{0,24},{1,25},{2,26},{3,27},{4,28},{5,29},{6,30},{7,31},{8,0},{9,1... | collective-permute-start | bytes 786440 | tf_op jit(solution)/shard_map/ppermute | solution.py:39
  22.3 4.6 %copy-done = bf16[384,128,128]{2,1,0:T(8,128)(2,1)S(1)} copy-done((bf16[384,128,128]{2,1,0:T(8,128)(2,1)S(1)}, bf16[384,128,128]{2,1,0:T(8,128)(2,1)}, u32[]{:S(2)}) %copy-start) | copy-done | bytes 12582936
  26.9 2.2 %weigh.4.refs_1_.refs_2_ = bf16[128,96,128]{2,1,0:T(8,128)(2,1)S(1)} custom-call(bf16[384,128,128]{2,1,0:T(8,128)(2,1)S(1)} %copy-done, f32[384,128]{1,0:T(8,128)S(1)} %get-tuple-element.19.weight_ref), custom_call_target="tpu_custom_call" | custom-call | bytes 25165824 | tf_op jit(solution)/shard_map/weigh/pallas_call | solution.py:99
  29.1 2.3 %weigh.5.refs_2_.refs_3_ = bf16[128,96,128]{2,1,0:T(8,128)(2,1)S(1)} custom-call(bf16[384,128,128]{2,1,0:T(8,128)(2,1)S(1)} %copy-done, f32[384,128]{1,0:T(8,128)S(1)} %get-tuple-element.19.weight_ref), custom_call_target="tpu_custom_call" | custom-call | bytes 25165824 | tf_op jit(solution)/shard_map/weigh/pallas_call | solution.py:99
  31.4 2.3 %weigh.6.refs_3_.refs_4_ = bf16[128,96,128]{2,1,0:T(8,128)(2,1)S(1)} custom-call(bf16[384,128,128]{2,1,0:T(8,128)(2,1)S(1)} %copy-done, f32[384,128]{1,0:T(8,128)S(1)} %get-tuple-element.19.weight_ref), custom_call_target="tpu_custom_call" | custom-call | bytes 25165824 | tf_op jit(solution)/shard_map/weigh/pallas_call | solution.py:99
  33.7 2.3 %weigh.7.refs_4_.refs_5_ = bf16[128,96,128]{2,1,0:T(8,128)(2,1)S(1)} custom-call(bf16[384,128,128]{2,1,0:T(8,128)(2,1)S(1)} %copy-done, f32[384,128]{1,0:T(8,128)S(1)} %get-tuple-element.19.weight_ref), custom_call_target="tpu_custom_call" | custom-call | bytes 25165824 | tf_op jit(solution)/shard_map/weigh/pallas_call | solution.py:99
  36.0 2.5 %collective-permute-start.4 = (bf16[32,32,128]{2,1,0:T(8,128)(2,1)S(1)}, bf16[32,32,128]{2,1,0:T(8,128)(2,1)S(1)}, u32[]{:S(2)}, u32[]{:S(2)}) collective-permute-start(bf16[32,32,128]{2,1,0:T(8,128)(2,1)S(1)} %constant_dynamic-update-slice_fusion.refs_0_), channel_id=1, source_target_pairs={{0,16},{1,17},{2,18},{3,19},{4,20},{5,21},{6,22},{7,23},{8,24},{9,... | collective-permute-start | bytes 786440 | tf_op jit(solution)/shard_map/ppermute | solution.py:39
  38.5 1.9 %correlate.2 = (f32[384,512]{1,0:T(8,128)S(1)}, f32[32,128]{1,0:T(8,128)S(1)}) custom-call(bf16[32,32,128]{2,1,0:T(8,128)(2,1)S(1)} %constant_dynamic-update-slice_fusion.refs_0_, bf16[128,96,128]{2,1,0:T(8,128)(2,1)S(1)} %weigh.4.refs_1_.refs_2_, bf16[128,96,128]{2,1,0:T(8,128)(2,1)S(1)} %weigh.5.refs_2_.refs_3_, ...), custom_call_target="tpu_custom_call" | custom-call | flops 1610612736 | tf_op jit(solution)/shard_map/correlate/pallas_call | solution.py:170
  40.5 3.6 %correlate.3 = (f32[384,512]{1,0:T(8,128)S(1)}, f32[32,128]{1,0:T(8,128)S(1)}) custom-call(bf16[32,32,128]{2,1,0:T(8,128)(2,1)S(1)} %collective-permute-done.5.refs_0_, bf16[32,32,128]{2,1,0:T(8,128)(2,1)S(1)} %collective-permute-done.6.refs_1_, bf16[128,96,128]{2,1,0:T(8,128)(2,1)S(1)} %weigh.4.refs_1_.refs_2_, ...), custom_call_target="tpu_custom_call" | custom-call | flops 3221225472 | tf_op jit(solution)/shard_map/correlate/pallas_call | solution.py:170
  44.1 2.4 %score.1 = (f32[384,512]{1,0:T(8,128)S(1)}, f32[16,384]{1,0:T(8,128)S(1)}) custom-call(bf16[32,32,128]{2,1,0:T(8,128)(2,1)S(1)} %collective-permute-done.4.refs_0_, bf16[128,96,128]{2,1,0:T(8,128)(2,1)S(1)} %weigh.4.refs_1_.refs_2_, bf16[128,96,128]{2,1,0:T(8,128)(2,1)S(1)} %weigh.5.refs_2_.refs_3_, bf16[128,96,128]{2,1,0:T(8,128)(2,1)S(1)} %weigh.6.refs_3_.refs_4_, ...), custom_call_target="tpu_custom_call" | custom-call | flops 1610612736 | tf_op jit(solution)/shard_map/score/pallas_call | solution.py:227
  51.8 2.6 %gather_sums.7 = bf16[33,32,128]{2,1,0:T(8,128)(2,1)S(1)} custom-call(bf16[512,384]{1,0:T(8,128)(2,1)S(1)} %get-tuple-element.27.refs_0_, bf16[128,96,128]{2,1,0:T(8,128)(2,1)S(1)} %weigh.4.refs_1_.refs_2_, bf16[128,96,128]{2,1,0:T(8,128)(2,1)S(1)} %weigh.5.refs_2_.refs_3_, bf16[128,96,128]{2,1,0:T(8,128)(2,1)S(1)} %weigh.6.refs_3_.refs_4_, ...), custom_call_target="tpu_custom_call" | custom-call | flops 1610612736 | tf_op jit(solution)/shard_map/gather_sums/pallas_call | solution.py:340
  54.4 2.6 %gather_sums.6 = bf16[33,32,128]{2,1,0:T(8,128)(2,1)S(1)} custom-call(bf16[512,384]{1,0:T(8,128)(2,1)S(1)} %get-tuple-element.27.refs_0_, bf16[128,96,128]{2,1,0:T(8,128)(2,1)S(1)} %weigh.4.refs_1_.refs_2_, bf16[128,96,128]{2,1,0:T(8,128)(2,1)S(1)} %weigh.5.refs_2_.refs_3_, bf16[128,96,128]{2,1,0:T(8,128)(2,1)S(1)} %weigh.6.refs_3_.refs_4_, ...), custom_call_target="tpu_custom_call" | custom-call | flops 1610612736 | tf_op jit(solution)/shard_map/gather_sums/pallas_call | solution.py:340
  57.1 2.6 %gather_sums.5 = bf16[33,32,128]{2,1,0:T(8,128)(2,1)S(1)} custom-call(bf16[512,384]{1,0:T(8,128)(2,1)S(1)} %get-tuple-element.27.refs_0_, bf16[128,96,128]{2,1,0:T(8,128)(2,1)S(1)} %weigh.4.refs_1_.refs_2_, bf16[128,96,128]{2,1,0:T(8,128)(2,1)S(1)} %weigh.5.refs_2_.refs_3_, bf16[128,96,128]{2,1,0:T(8,128)(2,1)S(1)} %weigh.6.refs_3_.refs_4_, ...), custom_call_target="tpu_custom_call" | custom-call | flops 1610612736 | tf_op jit(solution)/shard_map/gather_sums/pallas_call | solution.py:340
  59.7 3.3 %collective-permute-start.12 = (bf16[33,32,128]{2,1,0:T(8,128)(2,1)S(1)}, bf16[33,32,128]{2,1,0:T(8,128)(2,1)S(1)}, u32[]{:S(2)}, u32[]{:S(2)}) collective-permute-start(bf16[33,32,128]{2,1,0:T(8,128)(2,1)S(1)} %gather_sums.7), channel_id=1, source_target_pairs={{0,24},{1,25},{2,26},{3,27},{4,28},{5,29},{6,30},{7,31},{8,0},{9,1... | collective-permute-start | bytes 811016 | tf_op jit(solution)/shard_map/ppermute | solution.py:39
  64.6 2.6 %gather_sums.4.own_ref = f32[33,32,128]{2,1,0:T(8,128)S(1)} custom-call(bf16[512,384]{1,0:T(8,128)(2,1)S(1)} %get-tuple-element.27.refs_0_, bf16[128,96,128]{2,1,0:T(8,128)(2,1)S(1)} %weigh.4.refs_1_.refs_2_, bf16[128,96,128]{2,1,0:T(8,128)(2,1)S(1)} %weigh.5.refs_2_.refs_3_, bf16[128,96,128]{2,1,0:T(8,128)(2,1)S(1)} %weigh.6.refs_3_.refs_4_, ...), custom_call_target="tpu_custom_call" | custom-call | flops 1610612736 | tf_op jit(solution)/shard_map/gather_sums/pallas_call | solution.py:340
  67.2 7.7 %collective-permute-done.12.refs_2_ = bf16[33,32,128]{2,1,0:T(8,128)(2,1)S(1)} collective-permute-done((bf16[33,32,128]{2,1,0:T(8,128)(2,1)S(1)}, bf16[33,32,128]{2,1,0:T(8,128)(2,1)S(1)}, u32[]{:S(2)}, u32[]{:S(2)}) %collective-permute-start.12) | collective-permute-done | bytes 270368 | tf_op jit(solution)/shard_map/ppermute | solution.py:39
  74.9 3.4 %collective-permute-done.11.refs_1_ = bf16[33,32,128]{2,1,0:T(8,128)(2,1)S(1)} collective-permute-done((bf16[33,32,128]{2,1,0:T(8,128)(2,1)S(1)}, bf16[33,32,128]{2,1,0:T(8,128)(2,1)S(1)}, u32[]{:S(2)}, u32[]{:S(2)}) %collective-permute-start.11) | collective-permute-done | bytes 270368 | tf_op jit(solution)/shard_map/ppermute | solution.py:39
  78.6 2.0 %collective-permute-start.14 = (bf16[9,32,128]{2,1,0:T(8,128)(2,1)S(1)}, bf16[9,32,128]{2,1,0:T(8,128)(2,1)S(1)}, u32[]{:S(2)}, u32[]{:S(2)}) collective-permute-start(bf16[9,32,128]{2,1,0:T(8,128)(2,1)S(1)} %get-tuple-element.31), channel_id=1, source_target_pairs={{0,2},{1,3},{2,0},{3,1},{4,6},{5,7},{6,4},{7,5},{8,10},{9,11},{10,... | collective-permute-start | bytes 221192 | tf_op jit(solution)/shard_map/ppermute | solution.py:39
  80.6 1.9 %collective-permute-start.15 = (bf16[9,32,128]{2,1,0:T(8,128)(2,1)S(1)}, bf16[9,32,128]{2,1,0:T(8,128)(2,1)S(1)}, u32[]{:S(2)}, u32[]{:S(2)}) collective-permute-start(bf16[9,32,128]{2,1,0:T(8,128)(2,1)S(1)} %get-tuple-element.32), channel_id=1, source_target_pairs={{0,3},{1,0},{2,1},{3,2},{4,7},{5,4},{6,5},{7,6},{8,11},{9,8},{10,9... | collective-permute-start | bytes 221192 | tf_op jit(solution)/shard_map/ppermute | solution.py:39
  82.5 2.4 %collective-permute-done.13.refs_0_ = bf16[9,32,128]{2,1,0:T(8,128)(2,1)S(1)} collective-permute-done((bf16[9,32,128]{2,1,0:T(8,128)(2,1)S(1)}, bf16[9,32,128]{2,1,0:T(8,128)(2,1)S(1)}, u32[]{:S(2)}, u32[]{:S(2)}) %collective-permute-start.13) | collective-permute-done | bytes 73760 | tf_op jit(solution)/shard_map/ppermute | solution.py:39
  85.9 3.6 %collective-permute-start.16 = (bf16[5,32,128]{2,1,0:T(8,128)(2,1)S(1)}, bf16[5,32,128]{2,1,0:T(8,128)(2,1)S(1)}, u32[]{:S(2)}, u32[]{:S(2)}) collective-permute-start(bf16[5,32,128]{2,1,0:T(8,128)(2,1)S(1)} %get-tuple-element.34), channel_id=1, source_target_pairs={{0,4},{1,5},{2,6},{3,7},{4,0},{5,1},{6,2},{7,3},{8,12},{9,13},{10,... | collective-permute-start | bytes 122888 | tf_op jit(solution)/shard_map/ppermute | solution.py:39
  (45 shorter events, 18.9 us)
Async XLA Ops:
  1.4 5.9 %collective-permute-start = (bf16[4,32,128]{2,1,0:T(8,128)(2,1)S(1)}, bf16[4,32,128]{2,1,0:T(8,128)(2,1)S(1)}, u32[]{:S(2)}, u32[]{:S(2)}) collective-permute-start(bf16[4,32,128]{2,1,0:T(8,128)(2,1)S(1)} %bitcast.7), channel_id=1, source_target_pairs={{0,4},{1,5},{2,6},{3,7},{4,0},{5,1},{6,2},{7,3},{8,12},{9,13},{10,... | collective-permute-start | bytes 98312 | tf_op jit(solution)/shard_map/ppermute | solution.py:39
  7.3 5.0 %collective-permute-start.1 = (bf16[8,32,128]{2,1,0:T(8,128)(2,1)S(1)}, bf16[8,32,128]{2,1,0:T(8,128)(2,1)S(1)}, u32[]{:S(2)}, u32[]{:S(2)}) collective-permute-start(bf16[8,32,128]{2,1,0:T(8,128)(2,1)S(1)} %pad_maximum_fusion), channel_id=1, source_target_pairs={{0,3},{1,0},{2,1},{3,2},{4,7},{5,4},{6,5},{7,6},{8,11},{9,8},{10,9... | collective-permute-start | bytes 196616 | tf_op jit(solution)/shard_map/ppermute | solution.py:39
  10.3 5.8 %collective-permute-start.2 = (bf16[8,32,128]{2,1,0:T(8,128)(2,1)S(1)}, bf16[8,32,128]{2,1,0:T(8,128)(2,1)S(1)}, u32[]{:S(2)}, u32[]{:S(2)}) collective-permute-start(bf16[8,32,128]{2,1,0:T(8,128)(2,1)S(1)} %pad_maximum_fusion), channel_id=1, source_target_pairs={{0,2},{1,3},{2,0},{3,1},{4,6},{5,7},{6,4},{7,5},{8,10},{9,11},{10,... | collective-permute-start | bytes 196616 | tf_op jit(solution)/shard_map/ppermute | solution.py:39
  11.0 5.8 %collective-permute-start.3 = (bf16[8,32,128]{2,1,0:T(8,128)(2,1)S(1)}, bf16[8,32,128]{2,1,0:T(8,128)(2,1)S(1)}, u32[]{:S(2)}, u32[]{:S(2)}) collective-permute-start(bf16[8,32,128]{2,1,0:T(8,128)(2,1)S(1)} %pad_maximum_fusion), channel_id=1, source_target_pairs={{0,1},{1,2},{2,3},{3,0},{4,5},{5,6},{6,7},{7,4},{8,9},{9,10},{10,1... | collective-permute-start | bytes 196616 | tf_op jit(solution)/shard_map/ppermute | solution.py:39
  16.8 23.6 %collective-permute-start.5 = (bf16[32,32,128]{2,1,0:T(8,128)(2,1)S(1)}, bf16[32,32,128]{2,1,0:T(8,128)(2,1)S(1)}, u32[]{:S(2)}, u32[]{:S(2)}) collective-permute-start(bf16[32,32,128]{2,1,0:T(8,128)(2,1)S(1)} %constant_dynamic-update-slice_fusion.refs_0_), channel_id=1, source_target_pairs={{0,24},{1,25},{2,26},{3,27},{4,28},{5,29},{6,30},{7,31},{8,0},{9,1... | collective-permute-start | bytes 786440 | tf_op jit(solution)/shard_map/ppermute | solution.py:39
  19.7 20.8 %collective-permute-start.6 = (bf16[32,32,128]{2,1,0:T(8,128)(2,1)S(1)}, bf16[32,32,128]{2,1,0:T(8,128)(2,1)S(1)}, u32[]{:S(2)}, u32[]{:S(2)}) collective-permute-start(bf16[32,32,128]{2,1,0:T(8,128)(2,1)S(1)} %constant_dynamic-update-slice_fusion.refs_0_), channel_id=1, source_target_pairs={{0,8},{1,9},{2,10},{3,11},{4,12},{5,13},{6,14},{7,15},{8,16},{9,17... | collective-permute-start | bytes 786440 | tf_op jit(solution)/shard_map/ppermute | solution.py:39
  20.3 0.8 copy-start.1
  21.1 0.7 copy-start.2
  22.3 4.6 %copy-start = (bf16[384,128,128]{2,1,0:T(8,128)(2,1)S(1)}, bf16[384,128,128]{2,1,0:T(8,128)(2,1)}, u32[]{:S(2)}) copy-start(bf16[384,128,128]{2,1,0:T(8,128)(2,1)} %particles_ref.7) | copy-start | bytes 37748740
  33.7 2.3 %copy-start.3 = (s32[384]{0:T(512)S(1)}, s32[384]{0:T(512)}, u32[]{:S(2)}) copy-start(s32[384]{0:T(512)} %param.11) | copy-start | bytes 4612
  36.0 8.1 %collective-permute-start.4 = (bf16[32,32,128]{2,1,0:T(8,128)(2,1)S(1)}, bf16[32,32,128]{2,1,0:T(8,128)(2,1)S(1)}, u32[]{:S(2)}, u32[]{:S(2)}) collective-permute-start(bf16[32,32,128]{2,1,0:T(8,128)(2,1)S(1)} %constant_dynamic-update-slice_fusion.refs_0_), channel_id=1, source_target_pairs={{0,16},{1,17},{2,18},{3,19},{4,20},{5,21},{6,22},{7,23},{8,24},{9,... | collective-permute-start | bytes 786440 | tf_op jit(solution)/shard_map/ppermute | solution.py:39
  46.5 2.2 %collective-permute-start.7 = (f32[16,384]{1,0:T(8,128)S(1)}, f32[16,384]{1,0:T(8,128)S(1)}, u32[]{:S(2)}, u32[]{:S(2)}) collective-permute-start(f32[16,384]{1,0:T(8,128)S(1)} %get-tuple-element.26.own_ref), channel_id=1, source_target_pairs={{0,32},{32,0},{64,96},{96,64},{1,33},{33,1},{65,97},{97,65},{2,34}... | collective-permute-start | bytes 73736 | tf_op jit(solution)/shard_map/ppermute | solution.py:419
  46.6 3.9 %collective-permute-start.8 = (f32[16,384]{1,0:T(8,128)S(1)}, f32[16,384]{1,0:T(8,128)S(1)}, u32[]{:S(2)}, u32[]{:S(2)}) collective-permute-start(f32[16,384]{1,0:T(8,128)S(1)} %get-tuple-element.26.own_ref), channel_id=1, source_target_pairs={{0,64},{32,96},{64,0},{96,32},{1,65},{33,97},{65,1},{97,33},{2,66}... | collective-permute-start | bytes 73736 | tf_op jit(solution)/shard_map/ppermute | solution.py:419
  48.3 3.3 %collective-permute-start.9 = (f32[16,384]{1,0:T(8,128)S(1)}, f32[16,384]{1,0:T(8,128)S(1)}, u32[]{:S(2)}, u32[]{:S(2)}) collective-permute-start(f32[16,384]{1,0:T(8,128)S(1)} %get-tuple-element.26.own_ref), channel_id=1, source_target_pairs={{0,96},{32,64},{64,32},{96,0},{1,97},{33,65},{65,33},{97,1},{2,98}... | collective-permute-start | bytes 73736 | tf_op jit(solution)/shard_map/ppermute | solution.py:419
  59.7 15.2 %collective-permute-start.12 = (bf16[33,32,128]{2,1,0:T(8,128)(2,1)S(1)}, bf16[33,32,128]{2,1,0:T(8,128)(2,1)S(1)}, u32[]{:S(2)}, u32[]{:S(2)}) collective-permute-start(bf16[33,32,128]{2,1,0:T(8,128)(2,1)S(1)} %gather_sums.7), channel_id=1, source_target_pairs={{0,24},{1,25},{2,26},{3,27},{4,28},{5,29},{6,30},{7,31},{8,0},{9,1... | collective-permute-start | bytes 811016 | tf_op jit(solution)/shard_map/ppermute | solution.py:39
  63.0 15.3 %collective-permute-start.11 = (bf16[33,32,128]{2,1,0:T(8,128)(2,1)S(1)}, bf16[33,32,128]{2,1,0:T(8,128)(2,1)S(1)}, u32[]{:S(2)}, u32[]{:S(2)}) collective-permute-start(bf16[33,32,128]{2,1,0:T(8,128)(2,1)S(1)} %gather_sums.6), channel_id=1, source_target_pairs={{0,8},{1,9},{2,10},{3,11},{4,12},{5,13},{6,14},{7,15},{8,16},{9,17... | collective-permute-start | bytes 811016 | tf_op jit(solution)/shard_map/ppermute | solution.py:39
  63.0 15.3 %collective-permute-start.10 = (bf16[33,32,128]{2,1,0:T(8,128)(2,1)S(1)}, bf16[33,32,128]{2,1,0:T(8,128)(2,1)S(1)}, u32[]{:S(2)}, u32[]{:S(2)}) collective-permute-start(bf16[33,32,128]{2,1,0:T(8,128)(2,1)S(1)} %gather_sums.5), channel_id=1, source_target_pairs={{0,16},{1,17},{2,18},{3,19},{4,20},{5,21},{6,22},{7,23},{8,24},{9,... | collective-permute-start | bytes 811016 | tf_op jit(solution)/shard_map/ppermute | solution.py:39
  78.5 6.4 %collective-permute-start.13 = (bf16[9,32,128]{2,1,0:T(8,128)(2,1)S(1)}, bf16[9,32,128]{2,1,0:T(8,128)(2,1)S(1)}, u32[]{:S(2)}, u32[]{:S(2)}) collective-permute-start(bf16[9,32,128]{2,1,0:T(8,128)(2,1)S(1)} %get-tuple-element.30), channel_id=1, source_target_pairs={{0,1},{1,2},{2,3},{3,0},{4,5},{5,6},{6,7},{7,4},{8,9},{9,10},{10,1... | collective-permute-start | bytes 221192 | tf_op jit(solution)/shard_map/ppermute | solution.py:39
  78.6 6.3 %collective-permute-start.14 = (bf16[9,32,128]{2,1,0:T(8,128)(2,1)S(1)}, bf16[9,32,128]{2,1,0:T(8,128)(2,1)S(1)}, u32[]{:S(2)}, u32[]{:S(2)}) collective-permute-start(bf16[9,32,128]{2,1,0:T(8,128)(2,1)S(1)} %get-tuple-element.31), channel_id=1, source_target_pairs={{0,2},{1,3},{2,0},{3,1},{4,6},{5,7},{6,4},{7,5},{8,10},{9,11},{10,... | collective-permute-start | bytes 221192 | tf_op jit(solution)/shard_map/ppermute | solution.py:39
  80.6 5.2 %collective-permute-start.15 = (bf16[9,32,128]{2,1,0:T(8,128)(2,1)S(1)}, bf16[9,32,128]{2,1,0:T(8,128)(2,1)S(1)}, u32[]{:S(2)}, u32[]{:S(2)}) collective-permute-start(bf16[9,32,128]{2,1,0:T(8,128)(2,1)S(1)} %get-tuple-element.32), channel_id=1, source_target_pairs={{0,3},{1,0},{2,1},{3,2},{4,7},{5,4},{6,5},{7,6},{8,11},{9,8},{10,9... | collective-permute-start | bytes 221192 | tf_op jit(solution)/shard_map/ppermute | solution.py:39
  85.9 5.6 %collective-permute-start.16 = (bf16[5,32,128]{2,1,0:T(8,128)(2,1)S(1)}, bf16[5,32,128]{2,1,0:T(8,128)(2,1)S(1)}, u32[]{:S(2)}, u32[]{:S(2)}) collective-permute-start(bf16[5,32,128]{2,1,0:T(8,128)(2,1)S(1)} %get-tuple-element.34), channel_id=1, source_target_pairs={{0,4},{1,5},{2,6},{3,7},{4,0},{5,1},{6,2},{7,3},{8,12},{9,13},{10,... | collective-permute-start | bytes 122888 | tf_op jit(solution)/shard_map/ppermute | solution.py:39

commit v2 on v1

--- a/solution.py
+++ b/solution.py
@@ -12,7 +12,9 @@
 BF16 = jnp.bfloat16
 NX, NZ, NY = 4, 2, 4
 VMEM = pl.BlockSpec(memory_space=pltpu.VMEM)
+HBM = pl.BlockSpec(memory_space=pltpu.HBM)
 MIB = 2**20
+STREAMS = 1
 
 
 def params(mib):
@@ -20,7 +22,7 @@
 
 
 def cost(flops, nbytes):
-    return pl.CostEstimate(flops=flops, bytes_accessed=nbytes, transcendentals=0)
+    return pl.CostEstimate(flops=flops // 64, bytes_accessed=nbytes // 64, transcendentals=0)
 
 
 def coords(i):
@@ -45,25 +47,46 @@
     return high, low
 
 
-def setup_kernel(groups_ref, ctf_ref, noise_ref, weight_ref, power_ref):
+def load_rows(source, start, target, sems, first):
+    rows = target.shape[0] // STREAMS
+    return [
+        pltpu.make_async_copy(
+            source.at[pl.ds(start + i * rows, rows)], target.at[pl.ds(i * rows, rows)], sems.at[first + i]
+        )
+        for i in range(STREAMS)
+    ]
+
+
+def setup_kernel(groups_ref, ctf_hbm, noise_hbm, particles_hbm, weight_ref, power_ref, first_ref, ctf_ref, noise_ref, sems):
+    count = groups_ref.shape[0]
     group_count, cycles = ctf_ref.shape
-    count = groups_ref.shape[1]
+    copies = [
+        pltpu.make_async_copy(ctf_hbm, ctf_ref, sems.at[0]),
+        pltpu.make_async_copy(noise_hbm, noise_ref, sems.at[1]),
+    ]
+    copies += load_rows(particles_hbm, 0, first_ref, sems, 2)
+    for copy in copies:
+        copy.start()
     choose = (
-        lax.broadcasted_iota(jnp.int32, (group_count, count), 0) == groups_ref[...]
+        lax.broadcasted_iota(jnp.int32, (group_count, count), 0) == groups_ref[...].reshape(1, count)
     ).astype(F32)
     pick = lambda table: lax.dot_general(
         choose, table, (((0,), (0,)), ((), ())), precision=lax.Precision.HIGHEST,
         preferred_element_type=F32,
     )
+    copies[0].wait()
+    copies[1].wait()
     ctf = ctf_ref[...]
     noise = noise_ref[...]
     weight_ref[...] = pick(ctf) * noise
     high, low = split2(pick(ctf * ctf * noise))
     power_ref[:, :cycles] = high
     power_ref[:, cycles:] = low
-
-
-def setup(groups, ctf_table, noise_inv):
+    for copy in copies[2:]:
+        copy.wait()
+
+
+def setup(groups, ctf_table, noise_inv, particles, parts):
     count = groups.shape[0]
     cycles = ctf_table.shape[1]
     return pl.pallas_call(
@@ -71,45 +94,96 @@
         out_shape=(
             jax.ShapeDtypeStruct((count, cycles), F32),
             jax.ShapeDtypeStruct((count, 2 * cycles), BF16),
+            pltpu.VMEM((count // parts,) + particles.shape[1:], BF16),
         ),
-        in_specs=[VMEM] * 3,
-        out_specs=(VMEM, VMEM),
+        in_specs=[VMEM, HBM, HBM, HBM],
+        out_specs=(VMEM, VMEM, VMEM),
+        scratch_shapes=[
+            pltpu.VMEM(ctf_table.shape, F32),
+            pltpu.VMEM((1, cycles), F32),
+            pltpu.SemaphoreType.DMA((2 + STREAMS,)),
+        ],
         compiler_params=params(16),
         name="setup",
-    )(groups.reshape(1, count), ctf_table, noise_inv.reshape(1, cycles))
-
-
-def weigh_kernel(particles_ref, weight_ref, out_ref, wide):
-    rows, cycles, _ = particles_ref.shape
+    )(groups, ctf_table, noise_inv, particles)
+
+
+def weigh(particles, here, weight, part, parts):
+    count, cycles, angles = particles.shape
+    rows = count // parts
     pitch = cycles + 1
-    start = pl.multiple_of(pl.program_id(0) * rows, 16)
-    weight = weight_ref[...]
-    for n in range(rows):
-        wide[pl.ds(n * pitch, cycles), :] = particles_ref[n].astype(F32)
-    for q in range(cycles):
-        image = wide[pl.ds(q, rows, stride=pitch), :]
-        out_ref[q, pl.ds(start, rows), :] = (image * weight[:, q : q + 1]).astype(BF16)
-
-
-def weigh(particles, weight, part, parts):
-    count, cycles, angles = particles.shape
-    here = count // parts
-    rows = 48
-    steps = here // rows
-    return pl.pallas_call(
-        weigh_kernel,
-        out_shape=pltpu.VMEM((cycles, here, angles), BF16),
-        grid=(steps,),
-        in_specs=[
-            pl.BlockSpec((rows, cycles, angles), lambda i: (part * steps + i, 0, 0)),
-            pl.BlockSpec((rows, cycles), lambda i: (part * steps + i, 0)),
-        ],
+    last = part == parts - 1
+
+    def kernel(particles_hbm, here_ref, weight_ref, out_ref, token_ref, *refs):
+        if not last:
+            next_ref, wide, sems = refs
+            copies = load_rows(particles_hbm, (part + 1) * rows, next_ref, sems, 0)
+            for copy in copies:
+                copy.start()
+        else:
+            wide = refs[0]
+        values = weight_ref[part * rows : (part + 1) * rows]
+        token_ref[...] = values[0:8]
+        for n in range(rows):
+            wide[pl.ds(n * pitch, cycles), :] = here_ref[n].astype(F32)
+        pair = jnp.concatenate(split2(values), axis=1)
+        row = lax.broadcasted_iota(jnp.int32, (16, 2 * angles), 0)
+        side = lax.broadcasted_iota(jnp.int32, (16, 2 * angles), 1) // angles
+        for q in range(0, cycles, 2):
+            if q % 6 < 4:
+                base = q // 16 * 16
+                pick = [jnp.where(row - side == q % 16, 1.0, 0.0).astype(BF16)]
+                if base:
+                    pick = [jnp.zeros((base, 2 * angles), BF16)] + pick
+                if base + 16 < cycles:
+                    pick = pick + [jnp.zeros((cycles - 16 - base, 2 * angles), BF16)]
+                spread = jnp.dot(
+                    pair, jnp.concatenate(pick * 2, axis=0), preferred_element_type=F32
+                )
+                scales = [spread[:, :angles], spread[:, angles:]]
+            else:
+                scales = [values[:, q : q + 1], values[:, q + 1 : q + 2]]
+            for i in range(2):
+                image = wide[pl.ds(q + i, rows, stride=pitch), :]
+                out_ref[q + i] = (image * scales[i]).astype(BF16)
+        if not last:
+            for copy in copies:
+                copy.wait()
+
+    shape = (rows, cycles, angles)
+    return pl.pallas_call(
+        kernel,
+        out_shape=(pltpu.VMEM((cycles, rows, angles), BF16), jax.ShapeDtypeStruct((8, cycles), F32))
+        + (() if last else (pltpu.VMEM(shape, BF16),)),
+        in_specs=[HBM, VMEM, VMEM],
+        out_specs=(VMEM,) * (2 if last else 3),
+        scratch_shapes=[pltpu.VMEM((rows * pitch + 8, angles), F32)]
+        + ([] if last else [pltpu.SemaphoreType.DMA((STREAMS,))]),
+        compiler_params=params(16),
+        cost_estimate=cost(0, rows * cycles * angles * 16),
+        name="weigh",
+    )(particles, here, weight)
+
+
+def join(pieces, *tokens, turned=False):
+    rows, classes, angles = pieces[0].shape
+    if turned:
+        rows, classes = classes, rows
+
+    def kernel(*refs):
+        out_ref = refs[-1]
+        for i, ref in enumerate(refs[: len(pieces)]):
+            for j in range(rows):
+                out_ref[i * rows + j] = ref[:, j, :] if turned else ref[j]
+
+    return pl.pallas_call(
+        kernel,
+        out_shape=jax.ShapeDtypeStruct((rows * len(pieces), classes, angles), BF16),
+        in_specs=[VMEM] * len(pieces) + [pl.BlockSpec(memory_space=pl.ANY)] * len(tokens),
         out_specs=VMEM,
-        scratch_shapes=[pltpu.VMEM((rows * (cycles + 1) + 8, angles), F32)],
         compiler_params=params(16),
-        cost_estimate=cost(0, here * cycles * angles * 16),
-        name="weigh",
-    )(particles, weight)
+        name="join",
+    )(*pieces, *tokens)
 
 
 def cycle_of(dx, j):
@@ -376,45 +450,63 @@
         in_specs=[VMEM] * (1 + len(others)),
         out_specs=(VMEM,) * ways,
         compiler_params=params(16),
+        cost_estimate=cost(2 * 384 * 512 * 32 * 128, 0),
         name="add_parts",
     )(own, *others)
 
 
-def finish(own, other):
+def finish(own, others):
     rows, classes, angles = own.shape
 
-    def kernel(own_ref, other_ref, out_ref):
+    def kernel(own_ref, *refs):
+        others_ref, out_ref = refs[:-1], refs[-1]
         dom = lax.axis_index("dom")
         offset = ((dom // NY) % NZ) * (4 * NY) + (dom % NY) * 4
-        denom = join_denom(own_ref[rows - 1] + other_ref[rows - 1].astype(F32))
-        denom = pltpu.roll(denom, (angles - offset) % angles, 1) + TIKHONOV
+        denom = own_ref[rows - 1]
+        for ref in others_ref:
+            denom = denom + ref[rows - 1].astype(F32)
+        denom = pltpu.roll(join_denom(denom), (angles - offset) % angles, 1) + TIKHONOV
         for i in range(rows - 1):
-            numer = own_ref[i] + other_ref[i].astype(F32)
+            numer = own_ref[i]
+            for ref in others_ref:
+                numer = numer + ref[i].astype(F32)
             out_ref[:, i, :] = numer / denom[:, i : i + 1]
 
     return pl.pallas_call(
         kernel,
         out_shape=jax.ShapeDtypeStruct((classes, rows - 1, angles), F32),
-        in_specs=[VMEM, VMEM],
+        in_specs=[VMEM] * (1 + len(others)),
         out_specs=VMEM,
         compiler_params=params(16),
         name="finish",
-    )(own, other)
+    )(own, *others)
 
 
 def local(particles, references, ctf_table, noise_inv, groups, prior_rot):
     classes = references.shape[0]
-    piece = jnp.transpose(references, (1, 0, 2))
-    piece = jnp.concatenate([piece, send(piece, 0, 1, 0)], axis=0)
-    piece = jnp.concatenate([piece] + [send(piece, 0, 0, -d) for d in (1, 2, 3)], axis=0)
-    blocks = [piece] + [send(piece, -d, 0, 0) for d in (1, 2, 3)]
-
-    weight, power_pair = setup(groups, ctf_table, noise_inv)
     parts = 4
-    images = [weigh(particles, weight, part, parts) for part in range(parts)]
+    particles, ctf_table, noise_inv = (
+        pltpu.with_memory_space_constraint(value, pltpu.HBM)
+        for value in (particles, ctf_table, noise_inv.reshape(1, -1))
+    )
+    from_z = send(references, 0, 1, 0)
+    weight, power_pair, here = setup(groups, ctf_table, noise_inv, particles, parts)
+    piece = join([references, from_z], weight, turned=True)
+    from_y = [send(piece, 0, 0, -d) for d in (1, 2, 3)]
+    images = []
+    for part in range(parts):
+        image, token, *rest = weigh(particles, here, weight, part, parts)
+        here = rest[0] if rest else None
+        images.append(image)
+        if part == 1:
+            piece = join([piece] + from_y, token)
+        if part == 2:
+            late = join([piece], token)
+    blocks = [piece] + [send(late if d == 2 else piece, -d, 0, 0) for d in (1, 2, 3)]
 
     before = correlate((0,), blocks[:1], images, None)
-    before = correlate((1, 3), [blocks[1], blocks[3]], images, before)
+    before = correlate((3,), [blocks[3]], images, before)
+    before = correlate((1,), [blocks[1]], images, before)
     expo, stats = score((2,), [blocks[2]], images, before, power_pair, prior_rot)
     others = [lax.ppermute(stats, "cls", [(i, i ^ j) for i in range(4)]) for j in (1, 2, 3)]
     turned = turn_over(expo)
@@ -424,10 +516,12 @@
     for d in (2, 1, 3):
         arrived.append(send(gather_sums(d, resp, images, denom, BF16), d, 0, 0))
     own = gather_sums(0, resp, images, denom, F32)
-    pieces = add_parts(own, arrived, NY)
+    for value in arrived[:2]:
+        (own,) = add_parts(own, [value], 1)
+    pieces = add_parts(own, arrived[2:], NY)
     arrived = [send(pieces[d], 0, 0, d) for d in (1, 2, 3)]
     pieces = add_parts(pieces[0], arrived, NZ)
-    new_refs = finish(pieces[0], send(pieces[1], 0, 1, 0))
+    new_refs = finish(pieces[0], [send(pieces[1], 0, 1, 0)])
     return (new_refs, loglik[0])
 
 

time: 92.8 us -> 74.7 us (0.80)
  waiting for transfers between devices: 24.6 us -> 12.5 us
  local copies, waits for them, and re-layouts: 8.85 us -> 1.29 us
  Pallas kernels: 29.7 us -> 30.7 us
    ppermute x14, waiting for transfers between devices: 21.8 us -> 10.3 us  [send(): return lax.ppermute(value, 'dom', shift(dx, dz, dy))]
    unnamed x13 -> x6, local copies, waits for them, and re-layouts: 7.55 us -> 0.69 us
    pallas_call x1, Pallas kernels: 0.53 us -> 1.96 us  [setup(): pl.pallas_call(setup_kernel, out_shape=(jax.ShapeDtypeStruct((count, cycl...]
    pallas_call x4 -> x7, Pallas kernels: 9.03 us -> 7.87 us  [the longest x4 7.73 us: weigh(): pl.pallas_call(kernel, out_shape=(pltpu.VMEM((cycles, rows, angles), BF16...]
    pallas_call x2 -> x3, Pallas kernels: 5.48 us -> 5.87 us  [correlate(): pl.pallas_call(kernel, out_shape=(pltpu.VMEM((count, wide), F32), pltpu.V...]
  transfers between devices with their start and end apart: 17 -> 17, of which waited for: 12 -> 10; matrix products, arithmetic and copies ran while one was open for 2% -> 1% of each run, Pallas kernels for 19% -> 32%
where the time goes in v2:
time: 74.7 us; the launch traced here: 74.5 us
  Pallas kernels  30.7 us (41%)
  starting transfers between devices  29.1 us (39%)
  waiting for transfers between devices  12.5 us (17%)
  local copies, waits for them, and re-layouts  1.29 us (2%)
  between operations  0.86 us (1%)
    ppermute x14, starting transfers between devices, send(): return lax.ppermute(value, 'dom', shift(dx, dz, dy))  27.2 us
    pallas_call x4, Pallas kernels, gather_sums(): pl.pallas_call(kernel, out_shape=jax.ShapeDtypeStruct((length + 1, classe...  10.6 us
    ppermute x14, waiting for transfers between devices, send(): return lax.ppermute(value, 'dom', shift(dx, dz, dy))  10.3 us
    pallas_call x4, Pallas kernels, weigh(): pl.pallas_call(kernel, out_shape=(pltpu.VMEM((cycles, rows, angles), BF16...  7.73 us
    pallas_call x3, Pallas kernels, correlate(): pl.pallas_call(kernel, out_shape=(pltpu.VMEM((count, wide), F32), pltpu.V...  5.87 us
    pallas_call x1, Pallas kernels, score(): pl.pallas_call(kernel, out_shape=(pltpu.VMEM((count, wide), F32), jax.Sha...  2.47 us
    ppermute x3, waiting for transfers between devices, local(): lax.ppermute(stats, 'cls', [(i, i ^ j) for i in range(4)])  2.22 us
    pallas_call x1, Pallas kernels, setup(): pl.pallas_call(setup_kernel, out_shape=(jax.ShapeDtypeStruct((count, cycl...  1.96 us
  transfers between devices with their start and end apart: 17, of which 10 were waited for; matrix products, arithmetic and copies ran while one was open for 1% of the time, Pallas kernels for 32%

profile of v2, /device:TPU:0, one launch (start us, length us, event | category | flops | bytes accessed | tf_op | source)
XLA Modules:
  0.0 74.5 jit_solution(13796466604231191538)
XLA Ops:
  0.6 4.0 %collective-permute-start = (bf16[32,4,128]{2,1,0:T(4,128)(2,1)}, bf16[32,4,128]{2,1,0:T(4,128)(2,1)S(1)}, u32[]{:S(2)}, u32[]{:S(2)}) collective-permute-start(bf16[32,4,128]{2,1,0:T(4,128)(2,1)} %refs_0_.1), channel_id=1, source_target_pairs={{0,4},{1,5},{2,6},{3,7},{4,0},{5,1},{6,2},{7,3},{8,12},{9,13},{10,... | collective-permute-start | bytes 98312 | tf_op jit(solution)/shard_map/ppermute | solution.py:41
  5.4 2.0 %setup.1 = (f32[384,128]{1,0:T(8,128)S(1)}, bf16[384,256]{1,0:T(8,128)(2,1)S(1)}, bf16[96,128,128]{2,1,0:T(8,128)(2,1)S(1)}) custom-call(s32[384]{0:T(512)S(1)} %copy-done.1, f32[64,128]{1,0:T(8,128)} %ctf_hbm.1, f32[1,128]{1,0:T(1,128)} %bitcast.1, bf16[384,128,128]{2,1,0:T(8,128)(2,1)} %particles_hbm.9), custom_call_target="tpu_custom_call" | custom-call | tf_op jit(solution)/shard_map/setup/pallas_call | solution.py:92
  7.5 3.1 %collective-permute-start.1 = (bf16[8,32,128]{2,1,0:T(8,128)(2,1)S(1)}, bf16[8,32,128]{2,1,0:T(8,128)(2,1)S(1)}, u32[]{:S(2)}, u32[]{:S(2)}) collective-permute-start(bf16[8,32,128]{2,1,0:T(8,128)(2,1)S(1)} %join.3.refs_0_), channel_id=1, source_target_pairs={{0,3},{1,0},{2,1},{3,2},{4,7},{5,4},{6,5},{7,6},{8,11},{9,8},{10,9... | collective-permute-start | bytes 196616 | tf_op jit(solution)/shard_map/ppermute | solution.py:41
  12.1 2.5 %weigh.4 = (bf16[128,96,128]{2,1,0:T(8,128)(2,1)S(1)}, f32[8,128]{1,0:T(8,128)}, bf16[96,128,128]{2,1,0:T(8,128)(2,1)S(1)}) custom-call(bf16[384,128,128]{2,1,0:T(8,128)(2,1)} %particles_hbm.9, bf16[96,128,128]{2,1,0:T(8,128)(2,1)S(1)} %get-tuple-element.32.here_ref, f32[384,128]{1,0:T(8,128)S(1)} %get-tuple-element.31.refs_2_.weight_ref), custom_call_target="tpu_custom_call" | custom-call | bytes 393216 | tf_op jit(solution)/shard_map/weigh/pallas_call | solution.py:154
  14.6 1.9 %weigh.5 = (bf16[128,96,128]{2,1,0:T(8,128)(2,1)S(1)}, f32[8,128]{1,0:T(8,128)S(1)}, bf16[96,128,128]{2,1,0:T(8,128)(2,1)S(1)}) custom-call(bf16[384,128,128]{2,1,0:T(8,128)(2,1)} %particles_hbm.9, bf16[96,128,128]{2,1,0:T(8,128)(2,1)S(1)} %get-tuple-element.33.here_ref, f32[384,128]{1,0:T(8,128)S(1)} %get-tuple-element.31.refs_2_.weight_ref), custom_call_target="tpu_custom_call" | custom-call | bytes 393216 | tf_op jit(solution)/shard_map/weigh/pallas_call | solution.py:154
  18.6 1.7 %collective-permute-start.5 = (bf16[32,32,128]{2,1,0:T(8,128)(2,1)S(1)}, bf16[32,32,128]{2,1,0:T(8,128)(2,1)S(1)}, u32[]{:S(2)}, u32[]{:S(2)}) collective-permute-start(bf16[32,32,128]{2,1,0:T(8,128)(2,1)S(1)} %join.4.refs_0_), channel_id=1, source_target_pairs={{0,24},{1,25},{2,26},{3,27},{4,28},{5,29},{6,30},{7,31},{8,0},{9,1... | collective-permute-start | bytes 786440 | tf_op jit(solution)/shard_map/ppermute | solution.py:41
  20.3 1.9 %weigh.6 = (bf16[128,96,128]{2,1,0:T(8,128)(2,1)S(1)}, f32[8,128]{1,0:T(8,128)S(1)}, bf16[96,128,128]{2,1,0:T(8,128)(2,1)S(1)}) custom-call(bf16[384,128,128]{2,1,0:T(8,128)(2,1)} %particles_hbm.9, bf16[96,128,128]{2,1,0:T(8,128)(2,1)S(1)} %get-tuple-element.35.here_ref, f32[384,128]{1,0:T(8,128)S(1)} %get-tuple-element.31.refs_2_.weight_ref), custom_call_target="tpu_custom_call" | custom-call | bytes 393216 | tf_op jit(solution)/shard_map/weigh/pallas_call | solution.py:154
  22.3 2.1 %collective-permute-start.4 = (bf16[32,32,128]{2,1,0:T(8,128)(2,1)S(1)}, bf16[32,32,128]{2,1,0:T(8,128)(2,1)S(1)}, u32[]{:S(2)}, u32[]{:S(2)}) collective-permute-start(bf16[32,32,128]{2,1,0:T(8,128)(2,1)S(1)} %join.5), channel_id=1, source_target_pairs={{0,16},{1,17},{2,18},{3,19},{4,20},{5,21},{6,22},{7,23},{8,24},{9,... | collective-permute-start | bytes 786440 | tf_op jit(solution)/shard_map/ppermute | solution.py:41
  25.8 2.0 %correlate.3 = (f32[384,512]{1,0:T(8,128)S(1)}, f32[32,128]{1,0:T(8,128)S(1)}) custom-call(bf16[32,32,128]{2,1,0:T(8,128)(2,1)S(1)} %join.4.refs_0_, bf16[128,96,128]{2,1,0:T(8,128)(2,1)S(1)} %get-tuple-element.37.refs_1_, bf16[128,96,128]{2,1,0:T(8,128)(2,1)S(1)} %get-tuple-element.38.refs_2_, bf16[128,96,128]{2,1,0:T(8,128)(2,1)S(1)} %get-tuple-element.39.refs_3_, ...), custom_call_target="tpu_custom_call" | custom-call | flops 25165824 | tf_op jit(solution)/shard_map/correlate/pallas_call | solution.py:244
  27.8 2.0 %correlate.4 = (f32[384,512]{1,0:T(8,128)S(1)}, f32[32,128]{1,0:T(8,128)S(1)}) custom-call(bf16[32,32,128]{2,1,0:T(8,128)(2,1)S(1)} %collective-permute-done.6.refs_0_, bf16[128,96,128]{2,1,0:T(8,128)(2,1)S(1)} %get-tuple-element.37.refs_1_, bf16[128,96,128]{2,1,0:T(8,128)(2,1)S(1)} %get-tuple-element.38.refs_2_, ...), custom_call_target="tpu_custom_call" | custom-call | flops 25165824 | tf_op jit(solution)/shard_map/correlate/pallas_call | solution.py:244
  29.9 2.0 %correlate.5 = (f32[384,512]{1,0:T(8,128)S(1)}, f32[32,128]{1,0:T(8,128)S(1)}) custom-call(bf16[32,32,128]{2,1,0:T(8,128)(2,1)S(1)} %collective-permute-done.5.refs_0_, bf16[128,96,128]{2,1,0:T(8,128)(2,1)S(1)} %get-tuple-element.37.refs_1_, bf16[128,96,128]{2,1,0:T(8,128)(2,1)S(1)} %get-tuple-element.38.refs_2_, ...), custom_call_target="tpu_custom_call" | custom-call | flops 25165824 | tf_op jit(solution)/shard_map/correlate/pallas_call | solution.py:244
  31.9 2.5 %score.1 = (f32[384,512]{1,0:T(8,128)S(1)}, f32[16,384]{1,0:T(8,128)S(1)}) custom-call(bf16[32,32,128]{2,1,0:T(8,128)(2,1)S(1)} %collective-permute-done.4.refs_0_, bf16[128,96,128]{2,1,0:T(8,128)(2,1)S(1)} %get-tuple-element.37.refs_1_, bf16[128,96,128]{2,1,0:T(8,128)(2,1)S(1)} %get-tuple-element.38.refs_2_, ...), custom_call_target="tpu_custom_call" | custom-call | flops 25165824 | tf_op jit(solution)/shard_map/score/pallas_call | solution.py:301
  36.5 1.8 %collective-permute-done.8.b_ref = f32[16,384]{1,0:T(8,128)S(1)} collective-permute-done((f32[16,384]{1,0:T(8,128)S(1)}, f32[16,384]{1,0:T(8,128)S(1)}, u32[]{:S(2)}, u32[]{:S(2)}) %collective-permute-start.8) | collective-permute-done | bytes 24608 | tf_op jit(solution)/shard_map/ppermute | solution.py:511
  39.1 2.7 %gather_sums.5 = bf16[33,32,128]{2,1,0:T(8,128)(2,1)S(1)} custom-call(bf16[512,384]{1,0:T(8,128)(2,1)S(1)} %get-tuple-element.51.refs_0_, bf16[128,96,128]{2,1,0:T(8,128)(2,1)S(1)} %get-tuple-element.37.refs_1_, bf16[128,96,128]{2,1,0:T(8,128)(2,1)S(1)} %get-tuple-element.38.refs_2_, bf16[128,96,128]{2,1,0:T(8,128)(2,1)S(1)} %get-tuple-element.39.refs_3_, ...), custom_call_target="tpu_custom_call" | custom-call | flops 25165824 | tf_op jit(solution)/shard_map/gather_sums/pallas_call | solution.py:414
  43.5 2.7 %gather_sums.6 = bf16[33,32,128]{2,1,0:T(8,128)(2,1)S(1)} custom-call(bf16[512,384]{1,0:T(8,128)(2,1)S(1)} %get-tuple-element.51.refs_0_, bf16[128,96,128]{2,1,0:T(8,128)(2,1)S(1)} %get-tuple-element.37.refs_1_, bf16[128,96,128]{2,1,0:T(8,128)(2,1)S(1)} %get-tuple-element.38.refs_2_, bf16[128,96,128]{2,1,0:T(8,128)(2,1)S(1)} %get-tuple-element.39.refs_3_, ...), custom_call_target="tpu_custom_call" | custom-call | flops 25165824 | tf_op jit(solution)/shard_map/gather_sums/pallas_call | solution.py:414
  46.1 3.0 %collective-permute-start.11 = (bf16[33,32,128]{2,1,0:T(8,128)(2,1)S(1)}, bf16[33,32,128]{2,1,0:T(8,128)(2,1)S(1)}, u32[]{:S(2)}, u32[]{:S(2)}) collective-permute-start(bf16[33,32,128]{2,1,0:T(8,128)(2,1)S(1)} %gather_sums.6), channel_id=1, source_target_pairs={{0,8},{1,9},{2,10},{3,11},{4,12},{5,13},{6,14},{7,15},{8,16},{9,17... | collective-permute-start | bytes 811016 | tf_op jit(solution)/shard_map/ppermute | solution.py:41
  49.1 2.7 %gather_sums.7 = bf16[33,32,128]{2,1,0:T(8,128)(2,1)S(1)} custom-call(bf16[512,384]{1,0:T(8,128)(2,1)S(1)} %get-tuple-element.51.refs_0_, bf16[128,96,128]{2,1,0:T(8,128)(2,1)S(1)} %get-tuple-element.37.refs_1_, bf16[128,96,128]{2,1,0:T(8,128)(2,1)S(1)} %get-tuple-element.38.refs_2_, bf16[128,96,128]{2,1,0:T(8,128)(2,1)S(1)} %get-tuple-element.39.refs_3_, ...), custom_call_target="tpu_custom_call" | custom-call | flops 25165824 | tf_op jit(solution)/shard_map/gather_sums/pallas_call | solution.py:414
  52.2 2.6 %gather_sums.4.own_ref = f32[33,32,128]{2,1,0:T(8,128)S(1)} custom-call(bf16[512,384]{1,0:T(8,128)(2,1)S(1)} %get-tuple-element.51.refs_0_, bf16[128,96,128]{2,1,0:T(8,128)(2,1)S(1)} %get-tuple-element.37.refs_1_, bf16[128,96,128]{2,1,0:T(8,128)(2,1)S(1)} %get-tuple-element.38.refs_2_, bf16[128,96,128]{2,1,0:T(8,128)(2,1)S(1)} %get-tuple-element.39.refs_3_, ...), custom_call_target="tpu_custom_call" | custom-call | flops 25165824 | tf_op jit(solution)/shard_map/gather_sums/pallas_call | solution.py:414
  54.9 2.8 %collective-permute-done.11.refs_0_ = bf16[33,32,128]{2,1,0:T(8,128)(2,1)S(1)} collective-permute-done((bf16[33,32,128]{2,1,0:T(8,128)(2,1)S(1)}, bf16[33,32,128]{2,1,0:T(8,128)(2,1)S(1)}, u32[]{:S(2)}, u32[]{:S(2)}) %collective-permute-start.11) | collective-permute-done | bytes 270368 | tf_op jit(solution)/shard_map/ppermute | solution.py:41
  57.8 2.1 %collective-permute-done.12.refs_0_ = bf16[33,32,128]{2,1,0:T(8,128)(2,1)S(1)} collective-permute-done((bf16[33,32,128]{2,1,0:T(8,128)(2,1)S(1)}, bf16[33,32,128]{2,1,0:T(8,128)(2,1)S(1)}, u32[]{:S(2)}, u32[]{:S(2)}) %collective-permute-start.12) | collective-permute-done | bytes 270368 | tf_op jit(solution)/shard_map/ppermute | solution.py:41
  60.0 1.7 %collective-permute-start.13 = (bf16[9,32,128]{2,1,0:T(8,128)(2,1)S(1)}, bf16[9,32,128]{2,1,0:T(8,128)(2,1)S(1)}, u32[]{:S(2)}, u32[]{:S(2)}) collective-permute-start(bf16[9,32,128]{2,1,0:T(8,128)(2,1)S(1)} %get-tuple-element.54), channel_id=1, source_target_pairs={{0,1},{1,2},{2,3},{3,0},{4,5},{5,6},{6,7},{7,4},{8,9},{9,10},{10,1... | collective-permute-start | bytes 221192 | tf_op jit(solution)/shard_map/ppermute | solution.py:41
  61.7 1.8 %collective-permute-start.14 = (bf16[9,32,128]{2,1,0:T(8,128)(2,1)S(1)}, bf16[9,32,128]{2,1,0:T(8,128)(2,1)S(1)}, u32[]{:S(2)}, u32[]{:S(2)}) collective-permute-start(bf16[9,32,128]{2,1,0:T(8,128)(2,1)S(1)} %get-tuple-element.55), channel_id=1, source_target_pairs={{0,2},{1,3},{2,0},{3,1},{4,6},{5,7},{6,4},{7,5},{8,10},{9,11},{10,... | collective-permute-start | bytes 221192 | tf_op jit(solution)/shard_map/ppermute | solution.py:41
  65.8 1.8 %collective-permute-done.14.refs_1_ = bf16[9,32,128]{2,1,0:T(8,128)(2,1)S(1)} collective-permute-done((bf16[9,32,128]{2,1,0:T(8,128)(2,1)S(1)}, bf16[9,32,128]{2,1,0:T(8,128)(2,1)S(1)}, u32[]{:S(2)}, u32[]{:S(2)}) %collective-permute-start.14) | collective-permute-done | bytes 73760 | tf_op jit(solution)/shard_map/ppermute | solution.py:41
  68.1 3.3 %collective-permute-start.16 = (bf16[5,32,128]{2,1,0:T(8,128)(2,1)S(1)}, bf16[5,32,128]{2,1,0:T(8,128)(2,1)S(1)}, u32[]{:S(2)}, u32[]{:S(2)}) collective-permute-start(bf16[5,32,128]{2,1,0:T(8,128)(2,1)S(1)} %get-tuple-element.58), channel_id=1, source_target_pairs={{0,4},{1,5},{2,6},{3,7},{4,0},{5,1},{6,2},{7,3},{8,12},{9,13},{10,... | collective-permute-start | bytes 122888 | tf_op jit(solution)/shard_map/ppermute | solution.py:41
  (41 shorter events, 17.2 us)
Async XLA Ops:
  0.6 6.7 %collective-permute-start = (bf16[32,4,128]{2,1,0:T(4,128)(2,1)}, bf16[32,4,128]{2,1,0:T(4,128)(2,1)S(1)}, u32[]{:S(2)}, u32[]{:S(2)}) collective-permute-start(bf16[32,4,128]{2,1,0:T(4,128)(2,1)} %refs_0_.1), channel_id=1, source_target_pairs={{0,4},{1,5},{2,6},{3,7},{4,0},{5,1},{6,2},{7,3},{8,12},{9,13},{10,... | collective-permute-start | bytes 98312 | tf_op jit(solution)/shard_map/ppermute | solution.py:41
  4.7 0.7 copy-start.1
  5.4 2.0 %copy-start = (bf16[32,4,128]{2,1,0:T(4,128)(2,1)S(1)}, bf16[32,4,128]{2,1,0:T(4,128)(2,1)}, u32[]{:S(2)}) copy-start(bf16[32,4,128]{2,1,0:T(4,128)(2,1)} %refs_0_.1) | copy-start | bytes 98308
  7.5 9.1 %collective-permute-start.1 = (bf16[8,32,128]{2,1,0:T(8,128)(2,1)S(1)}, bf16[8,32,128]{2,1,0:T(8,128)(2,1)S(1)}, u32[]{:S(2)}, u32[]{:S(2)}) collective-permute-start(bf16[8,32,128]{2,1,0:T(8,128)(2,1)S(1)} %join.3.refs_0_), channel_id=1, source_target_pairs={{0,3},{1,0},{2,1},{3,2},{4,7},{5,4},{6,5},{7,6},{8,11},{9,8},{10,9... | collective-permute-start | bytes 196616 | tf_op jit(solution)/shard_map/ppermute | solution.py:41
  10.5 6.0 %collective-permute-start.2 = (bf16[8,32,128]{2,1,0:T(8,128)(2,1)S(1)}, bf16[8,32,128]{2,1,0:T(8,128)(2,1)S(1)}, u32[]{:S(2)}, u32[]{:S(2)}) collective-permute-start(bf16[8,32,128]{2,1,0:T(8,128)(2,1)S(1)} %join.3.refs_0_), channel_id=1, source_target_pairs={{0,2},{1,3},{2,0},{3,1},{4,6},{5,7},{6,4},{7,5},{8,10},{9,11},{10,... | collective-permute-start | bytes 196616 | tf_op jit(solution)/shard_map/ppermute | solution.py:41
  11.2 5.8 %collective-permute-start.3 = (bf16[8,32,128]{2,1,0:T(8,128)(2,1)S(1)}, bf16[8,32,128]{2,1,0:T(8,128)(2,1)S(1)}, u32[]{:S(2)}, u32[]{:S(2)}) collective-permute-start(bf16[8,32,128]{2,1,0:T(8,128)(2,1)S(1)} %join.3.refs_0_), channel_id=1, source_target_pairs={{0,1},{1,2},{2,3},{3,0},{4,5},{5,6},{6,7},{7,4},{8,9},{9,10},{10,1... | collective-permute-start | bytes 196616 | tf_op jit(solution)/shard_map/ppermute | solution.py:41
  17.0 10.7 %collective-permute-start.6 = (bf16[32,32,128]{2,1,0:T(8,128)(2,1)S(1)}, bf16[32,32,128]{2,1,0:T(8,128)(2,1)S(1)}, u32[]{:S(2)}, u32[]{:S(2)}) collective-permute-start(bf16[32,32,128]{2,1,0:T(8,128)(2,1)S(1)} %join.4.refs_0_), channel_id=1, source_target_pairs={{0,8},{1,9},{2,10},{3,11},{4,12},{5,13},{6,14},{7,15},{8,16},{9,17... | collective-permute-start | bytes 786440 | tf_op jit(solution)/shard_map/ppermute | solution.py:41
  18.6 11.3 %collective-permute-start.5 = (bf16[32,32,128]{2,1,0:T(8,128)(2,1)S(1)}, bf16[32,32,128]{2,1,0:T(8,128)(2,1)S(1)}, u32[]{:S(2)}, u32[]{:S(2)}) collective-permute-start(bf16[32,32,128]{2,1,0:T(8,128)(2,1)S(1)} %join.4.refs_0_), channel_id=1, source_target_pairs={{0,24},{1,25},{2,26},{3,27},{4,28},{5,29},{6,30},{7,31},{8,0},{9,1... | collective-permute-start | bytes 786440 | tf_op jit(solution)/shard_map/ppermute | solution.py:41
  22.3 9.6 %collective-permute-start.4 = (bf16[32,32,128]{2,1,0:T(8,128)(2,1)S(1)}, bf16[32,32,128]{2,1,0:T(8,128)(2,1)S(1)}, u32[]{:S(2)}, u32[]{:S(2)}) collective-permute-start(bf16[32,32,128]{2,1,0:T(8,128)(2,1)S(1)} %join.5), channel_id=1, source_target_pairs={{0,16},{1,17},{2,18},{3,19},{4,20},{5,21},{6,22},{7,23},{8,24},{9,... | collective-permute-start | bytes 786440 | tf_op jit(solution)/shard_map/ppermute | solution.py:41
  24.3 1.4 %copy-start.2 = (s32[384]{0:T(512)S(1)}, s32[384]{0:T(512)}, u32[]{:S(2)}) copy-start(s32[384]{0:T(512)} %param.11) | copy-start | bytes 4612
  34.3 2.2 %collective-permute-start.7 = (f32[16,384]{1,0:T(8,128)S(1)}, f32[16,384]{1,0:T(8,128)S(1)}, u32[]{:S(2)}, u32[]{:S(2)}) collective-permute-start(f32[16,384]{1,0:T(8,128)S(1)} %get-tuple-element.50.own_ref), channel_id=1, source_target_pairs={{0,32},{32,0},{64,96},{96,64},{1,33},{33,1},{65,97},{97,65},{2,34}... | collective-permute-start | bytes 73736 | tf_op jit(solution)/shard_map/ppermute | solution.py:511
  34.4 3.9 %collective-permute-start.8 = (f32[16,384]{1,0:T(8,128)S(1)}, f32[16,384]{1,0:T(8,128)S(1)}, u32[]{:S(2)}, u32[]{:S(2)}) collective-permute-start(f32[16,384]{1,0:T(8,128)S(1)} %get-tuple-element.50.own_ref), channel_id=1, source_target_pairs={{0,64},{32,96},{64,0},{96,32},{1,65},{33,97},{65,1},{97,33},{2,66}... | collective-permute-start | bytes 73736 | tf_op jit(solution)/shard_map/ppermute | solution.py:511
  35.5 3.3 %collective-permute-start.9 = (f32[16,384]{1,0:T(8,128)S(1)}, f32[16,384]{1,0:T(8,128)S(1)}, u32[]{:S(2)}, u32[]{:S(2)}) collective-permute-start(f32[16,384]{1,0:T(8,128)S(1)} %get-tuple-element.50.own_ref), channel_id=1, source_target_pairs={{0,96},{32,64},{64,32},{96,0},{1,97},{33,65},{65,33},{97,1},{2,98}... | collective-permute-start | bytes 73736 | tf_op jit(solution)/shard_map/ppermute | solution.py:511
  41.8 13.0 %collective-permute-start.10 = (bf16[33,32,128]{2,1,0:T(8,128)(2,1)S(1)}, bf16[33,32,128]{2,1,0:T(8,128)(2,1)S(1)}, u32[]{:S(2)}, u32[]{:S(2)}) collective-permute-start(bf16[33,32,128]{2,1,0:T(8,128)(2,1)S(1)} %gather_sums.5), channel_id=1, source_target_pairs={{0,16},{1,17},{2,18},{3,19},{4,20},{5,21},{6,22},{7,23},{8,24},{9,... | collective-permute-start | bytes 811016 | tf_op jit(solution)/shard_map/ppermute | solution.py:41
  46.1 11.6 %collective-permute-start.11 = (bf16[33,32,128]{2,1,0:T(8,128)(2,1)S(1)}, bf16[33,32,128]{2,1,0:T(8,128)(2,1)S(1)}, u32[]{:S(2)}, u32[]{:S(2)}) collective-permute-start(bf16[33,32,128]{2,1,0:T(8,128)(2,1)S(1)} %gather_sums.6), channel_id=1, source_target_pairs={{0,8},{1,9},{2,10},{3,11},{4,12},{5,13},{6,14},{7,15},{8,16},{9,17... | collective-permute-start | bytes 811016 | tf_op jit(solution)/shard_map/ppermute | solution.py:41
  51.8 8.0 %collective-permute-start.12 = (bf16[33,32,128]{2,1,0:T(8,128)(2,1)S(1)}, bf16[33,32,128]{2,1,0:T(8,128)(2,1)S(1)}, u32[]{:S(2)}, u32[]{:S(2)}) collective-permute-start(bf16[33,32,128]{2,1,0:T(8,128)(2,1)S(1)} %gather_sums.7), channel_id=1, source_target_pairs={{0,24},{1,25},{2,26},{3,27},{4,28},{5,29},{6,30},{7,31},{8,0},{9,1... | collective-permute-start | bytes 811016 | tf_op jit(solution)/shard_map/ppermute | solution.py:41
  60.0 5.8 %collective-permute-start.13 = (bf16[9,32,128]{2,1,0:T(8,128)(2,1)S(1)}, bf16[9,32,128]{2,1,0:T(8,128)(2,1)S(1)}, u32[]{:S(2)}, u32[]{:S(2)}) collective-permute-start(bf16[9,32,128]{2,1,0:T(8,128)(2,1)S(1)} %get-tuple-element.54), channel_id=1, source_target_pairs={{0,1},{1,2},{2,3},{3,0},{4,5},{5,6},{6,7},{7,4},{8,9},{9,10},{10,1... | collective-permute-start | bytes 221192 | tf_op jit(solution)/shard_map/ppermute | solution.py:41
  61.7 5.9 %collective-permute-start.14 = (bf16[9,32,128]{2,1,0:T(8,128)(2,1)S(1)}, bf16[9,32,128]{2,1,0:T(8,128)(2,1)S(1)}, u32[]{:S(2)}, u32[]{:S(2)}) collective-permute-start(bf16[9,32,128]{2,1,0:T(8,128)(2,1)S(1)} %get-tuple-element.55), channel_id=1, source_target_pairs={{0,2},{1,3},{2,0},{3,1},{4,6},{5,7},{6,4},{7,5},{8,10},{9,11},{10,... | collective-permute-start | bytes 221192 | tf_op jit(solution)/shard_map/ppermute | solution.py:41
  63.6 4.4 %collective-permute-start.15 = (bf16[9,32,128]{2,1,0:T(8,128)(2,1)S(1)}, bf16[9,32,128]{2,1,0:T(8,128)(2,1)S(1)}, u32[]{:S(2)}, u32[]{:S(2)}) collective-permute-start(bf16[9,32,128]{2,1,0:T(8,128)(2,1)S(1)} %get-tuple-element.56), channel_id=1, source_target_pairs={{0,3},{1,0},{2,1},{3,2},{4,7},{5,4},{6,5},{7,6},{8,11},{9,8},{10,9... | collective-permute-start | bytes 221192 | tf_op jit(solution)/shard_map/ppermute | solution.py:41
  68.1 5.5 %collective-permute-start.16 = (bf16[5,32,128]{2,1,0:T(8,128)(2,1)S(1)}, bf16[5,32,128]{2,1,0:T(8,128)(2,1)S(1)}, u32[]{:S(2)}, u32[]{:S(2)}) collective-permute-start(bf16[5,32,128]{2,1,0:T(8,128)(2,1)S(1)} %get-tuple-element.58), channel_id=1, source_target_pairs={{0,4},{1,5},{2,6},{3,7},{4,0},{5,1},{6,2},{7,3},{8,12},{9,13},{10,... | collective-permute-start | bytes 122888 | tf_op jit(solution)/shard_map/ppermute | solution.py:41

commit v3 on v2

--- a/solution.py
+++ b/solution.py
@@ -502,12 +502,12 @@
             piece = join([piece] + from_y, token)
         if part == 2:
             late = join([piece], token)
-    blocks = [piece] + [send(late if d == 2 else piece, -d, 0, 0) for d in (1, 2, 3)]
+    blocks = [piece] + [send(late if d == 1 else piece, -d, 0, 0) for d in (1, 2, 3)]
 
     before = correlate((0,), blocks[:1], images, None)
     before = correlate((3,), [blocks[3]], images, before)
-    before = correlate((1,), [blocks[1]], images, before)
-    expo, stats = score((2,), [blocks[2]], images, before, power_pair, prior_rot)
+    before = correlate((2,), [blocks[2]], images, before)
+    expo, stats = score((1,), [blocks[1]], images, before, power_pair, prior_rot)
     others = [lax.ppermute(stats, "cls", [(i, i ^ j) for i in range(4)]) for j in (1, 2, 3)]
     turned = turn_over(expo)
     resp, loglik, denom = share(turned, stats, others, power_pair, classes)

time: 74.7 us -> 74.4 us (level)
  transfers between devices with their start and end apart: 17 -> 17, of which waited for: 10 -> 9; matrix products, arithmetic and copies ran while one was open for 1% -> 1% of each run, Pallas kernels for 32% -> 32%
where the time goes in v3:
time: 74.4 us; the launch traced here: 74.1 us
  Pallas kernels  30.7 us (41%)
  starting transfers between devices  28.5 us (38%)
  waiting for transfers between devices  12.8 us (17%)
  local copies, waits for them, and re-layouts  1.29 us (2%)
  between operations  0.86 us (1%)
    ppermute x14, starting transfers between devices, send(): return lax.ppermute(value, 'dom', shift(dx, dz, dy))  26.5 us
    pallas_call x4, Pallas kernels, gather_sums(): pl.pallas_call(kernel, out_shape=jax.ShapeDtypeStruct((length + 1, classe...  10.6 us
    ppermute x14, waiting for transfers between devices, send(): return lax.ppermute(value, 'dom', shift(dx, dz, dy))  10.6 us
    pallas_call x4, Pallas kernels, weigh(): pl.pallas_call(kernel, out_shape=(pltpu.VMEM((cycles, rows, angles), BF16...  7.72 us
    pallas_call x3, Pallas kernels, correlate(): pl.pallas_call(kernel, out_shape=(pltpu.VMEM((count, wide), F32), pltpu.V...  5.87 us
    pallas_call x1, Pallas kernels, score(): pl.pallas_call(kernel, out_shape=(pltpu.VMEM((count, wide), F32), jax.Sha...  2.47 us
    ppermute x3, waiting for transfers between devices, local(): lax.ppermute(stats, 'cls', [(i, i ^ j) for i in range(4)])  2.21 us
    pallas_call x1, Pallas kernels, setup(): pl.pallas_call(setup_kernel, out_shape=(jax.ShapeDtypeStruct((count, cycl...  1.96 us
  transfers between devices with their start and end apart: 17, of which 9 were waited for; matrix products, arithmetic and copies ran while one was open for 1% of the time, Pallas kernels for 32%

profile of v3, /device:TPU:0, one launch (start us, length us, event | category | flops | bytes accessed | tf_op | source)
XLA Modules:
  0.0 74.1 jit_solution(1136688877215558284)
XLA Ops:
  0.6 4.0 %collective-permute-start = (bf16[32,4,128]{2,1,0:T(4,128)(2,1)}, bf16[32,4,128]{2,1,0:T(4,128)(2,1)S(1)}, u32[]{:S(2)}, u32[]{:S(2)}) collective-permute-start(bf16[32,4,128]{2,1,0:T(4,128)(2,1)} %refs_0_.1), channel_id=1, source_target_pairs={{0,4},{1,5},{2,6},{3,7},{4,0},{5,1},{6,2},{7,3},{8,12},{9,13},{10,... | collective-permute-start | bytes 98312 | tf_op jit(solution)/shard_map/ppermute | solution.py:41
  5.4 2.0 %setup.1 = (f32[384,128]{1,0:T(8,128)S(1)}, bf16[384,256]{1,0:T(8,128)(2,1)S(1)}, bf16[96,128,128]{2,1,0:T(8,128)(2,1)S(1)}) custom-call(s32[384]{0:T(512)S(1)} %copy-done.1, f32[64,128]{1,0:T(8,128)} %ctf_hbm.1, f32[1,128]{1,0:T(1,128)} %bitcast.1, bf16[384,128,128]{2,1,0:T(8,128)(2,1)} %particles_hbm.9), custom_call_target="tpu_custom_call" | custom-call | tf_op jit(solution)/shard_map/setup/pallas_call | solution.py:92
  7.5 3.1 %collective-permute-start.1 = (bf16[8,32,128]{2,1,0:T(8,128)(2,1)S(1)}, bf16[8,32,128]{2,1,0:T(8,128)(2,1)S(1)}, u32[]{:S(2)}, u32[]{:S(2)}) collective-permute-start(bf16[8,32,128]{2,1,0:T(8,128)(2,1)S(1)} %join.3.refs_0_), channel_id=1, source_target_pairs={{0,3},{1,0},{2,1},{3,2},{4,7},{5,4},{6,5},{7,6},{8,11},{9,8},{10,9... | collective-permute-start | bytes 196616 | tf_op jit(solution)/shard_map/ppermute | solution.py:41
  12.1 2.5 %weigh.4 = (bf16[128,96,128]{2,1,0:T(8,128)(2,1)S(1)}, f32[8,128]{1,0:T(8,128)}, bf16[96,128,128]{2,1,0:T(8,128)(2,1)S(1)}) custom-call(bf16[384,128,128]{2,1,0:T(8,128)(2,1)} %particles_hbm.9, bf16[96,128,128]{2,1,0:T(8,128)(2,1)S(1)} %get-tuple-element.32.here_ref, f32[384,128]{1,0:T(8,128)S(1)} %get-tuple-element.31.refs_2_.weight_ref), custom_call_target="tpu_custom_call" | custom-call | bytes 393216 | tf_op jit(solution)/shard_map/weigh/pallas_call | solution.py:154
  14.6 1.9 %weigh.5 = (bf16[128,96,128]{2,1,0:T(8,128)(2,1)S(1)}, f32[8,128]{1,0:T(8,128)S(1)}, bf16[96,128,128]{2,1,0:T(8,128)(2,1)S(1)}) custom-call(bf16[384,128,128]{2,1,0:T(8,128)(2,1)} %particles_hbm.9, bf16[96,128,128]{2,1,0:T(8,128)(2,1)S(1)} %get-tuple-element.33.here_ref, f32[384,128]{1,0:T(8,128)S(1)} %get-tuple-element.31.refs_2_.weight_ref), custom_call_target="tpu_custom_call" | custom-call | bytes 393216 | tf_op jit(solution)/shard_map/weigh/pallas_call | solution.py:154
  18.6 2.7 %collective-permute-start.5 = (bf16[32,32,128]{2,1,0:T(8,128)(2,1)S(1)}, bf16[32,32,128]{2,1,0:T(8,128)(2,1)S(1)}, u32[]{:S(2)}, u32[]{:S(2)}) collective-permute-start(bf16[32,32,128]{2,1,0:T(8,128)(2,1)S(1)} %join.4.refs_0_), channel_id=1, source_target_pairs={{0,16},{1,17},{2,18},{3,19},{4,20},{5,21},{6,22},{7,23},{8,24},{9,... | collective-permute-start | bytes 786440 | tf_op jit(solution)/shard_map/ppermute | solution.py:41
  21.3 1.9 %weigh.6 = (bf16[128,96,128]{2,1,0:T(8,128)(2,1)S(1)}, f32[8,128]{1,0:T(8,128)S(1)}, bf16[96,128,128]{2,1,0:T(8,128)(2,1)S(1)}) custom-call(bf16[384,128,128]{2,1,0:T(8,128)(2,1)} %particles_hbm.9, bf16[96,128,128]{2,1,0:T(8,128)(2,1)S(1)} %get-tuple-element.35.here_ref, f32[384,128]{1,0:T(8,128)S(1)} %get-tuple-element.31.refs_2_.weight_ref), custom_call_target="tpu_custom_call" | custom-call | bytes 393216 | tf_op jit(solution)/shard_map/weigh/pallas_call | solution.py:154
  23.3 1.7 %collective-permute-start.4 = (bf16[32,32,128]{2,1,0:T(8,128)(2,1)S(1)}, bf16[32,32,128]{2,1,0:T(8,128)(2,1)S(1)}, u32[]{:S(2)}, u32[]{:S(2)}) collective-permute-start(bf16[32,32,128]{2,1,0:T(8,128)(2,1)S(1)} %join.5), channel_id=1, source_target_pairs={{0,24},{1,25},{2,26},{3,27},{4,28},{5,29},{6,30},{7,31},{8,0},{9,1... | collective-permute-start | bytes 786440 | tf_op jit(solution)/shard_map/ppermute | solution.py:41
  26.4 2.0 %correlate.3 = (f32[384,512]{1,0:T(8,128)S(1)}, f32[32,128]{1,0:T(8,128)S(1)}) custom-call(bf16[32,32,128]{2,1,0:T(8,128)(2,1)S(1)} %join.4.refs_0_, bf16[128,96,128]{2,1,0:T(8,128)(2,1)S(1)} %get-tuple-element.37.refs_1_, bf16[128,96,128]{2,1,0:T(8,128)(2,1)S(1)} %get-tuple-element.38.refs_2_, bf16[128,96,128]{2,1,0:T(8,128)(2,1)S(1)} %get-tuple-element.39.refs_3_, ...), custom_call_target="tpu_custom_call" | custom-call | flops 25165824 | tf_op jit(solution)/shard_map/correlate/pallas_call | solution.py:244
  28.4 2.0 %correlate.4 = (f32[384,512]{1,0:T(8,128)S(1)}, f32[32,128]{1,0:T(8,128)S(1)}) custom-call(bf16[32,32,128]{2,1,0:T(8,128)(2,1)S(1)} %collective-permute-done.6.refs_0_, bf16[128,96,128]{2,1,0:T(8,128)(2,1)S(1)} %get-tuple-element.37.refs_1_, bf16[128,96,128]{2,1,0:T(8,128)(2,1)S(1)} %get-tuple-element.38.refs_2_, ...), custom_call_target="tpu_custom_call" | custom-call | flops 25165824 | tf_op jit(solution)/shard_map/correlate/pallas_call | solution.py:244
  31.4 2.0 %correlate.5 = (f32[384,512]{1,0:T(8,128)S(1)}, f32[32,128]{1,0:T(8,128)S(1)}) custom-call(bf16[32,32,128]{2,1,0:T(8,128)(2,1)S(1)} %collective-permute-done.5.refs_0_, bf16[128,96,128]{2,1,0:T(8,128)(2,1)S(1)} %get-tuple-element.37.refs_1_, bf16[128,96,128]{2,1,0:T(8,128)(2,1)S(1)} %get-tuple-element.38.refs_2_, ...), custom_call_target="tpu_custom_call" | custom-call | flops 25165824 | tf_op jit(solution)/shard_map/correlate/pallas_call | solution.py:244
  33.4 2.5 %score.1 = (f32[384,512]{1,0:T(8,128)S(1)}, f32[16,384]{1,0:T(8,128)S(1)}) custom-call(bf16[32,32,128]{2,1,0:T(8,128)(2,1)S(1)} %collective-permute-done.4.refs_0_, bf16[128,96,128]{2,1,0:T(8,128)(2,1)S(1)} %get-tuple-element.37.refs_1_, bf16[128,96,128]{2,1,0:T(8,128)(2,1)S(1)} %get-tuple-element.38.refs_2_, ...), custom_call_target="tpu_custom_call" | custom-call | flops 25165824 | tf_op jit(solution)/shard_map/score/pallas_call | solution.py:301
  38.1 1.8 %collective-permute-done.8.b_ref = f32[16,384]{1,0:T(8,128)S(1)} collective-permute-done((f32[16,384]{1,0:T(8,128)S(1)}, f32[16,384]{1,0:T(8,128)S(1)}, u32[]{:S(2)}, u32[]{:S(2)}) %collective-permute-start.8) | collective-permute-done | bytes 24608 | tf_op jit(solution)/shard_map/ppermute | solution.py:511
  40.6 2.7 %gather_sums.5 = bf16[33,32,128]{2,1,0:T(8,128)(2,1)S(1)} custom-call(bf16[512,384]{1,0:T(8,128)(2,1)S(1)} %get-tuple-element.51.refs_0_, bf16[128,96,128]{2,1,0:T(8,128)(2,1)S(1)} %get-tuple-element.37.refs_1_, bf16[128,96,128]{2,1,0:T(8,128)(2,1)S(1)} %get-tuple-element.38.refs_2_, bf16[128,96,128]{2,1,0:T(8,128)(2,1)S(1)} %get-tuple-element.39.refs_3_, ...), custom_call_target="tpu_custom_call" | custom-call | flops 25165824 | tf_op jit(solution)/shard_map/gather_sums/pallas_call | solution.py:414
  44.2 2.7 %gather_sums.6 = bf16[33,32,128]{2,1,0:T(8,128)(2,1)S(1)} custom-call(bf16[512,384]{1,0:T(8,128)(2,1)S(1)} %get-tuple-element.51.refs_0_, bf16[128,96,128]{2,1,0:T(8,128)(2,1)S(1)} %get-tuple-element.37.refs_1_, bf16[128,96,128]{2,1,0:T(8,128)(2,1)S(1)} %get-tuple-element.38.refs_2_, bf16[128,96,128]{2,1,0:T(8,128)(2,1)S(1)} %get-tuple-element.39.refs_3_, ...), custom_call_target="tpu_custom_call" | custom-call | flops 25165824 | tf_op jit(solution)/shard_map/gather_sums/pallas_call | solution.py:414
  47.4 2.7 %gather_sums.7 = bf16[33,32,128]{2,1,0:T(8,128)(2,1)S(1)} custom-call(bf16[512,384]{1,0:T(8,128)(2,1)S(1)} %get-tuple-element.51.refs_0_, bf16[128,96,128]{2,1,0:T(8,128)(2,1)S(1)} %get-tuple-element.37.refs_1_, bf16[128,96,128]{2,1,0:T(8,128)(2,1)S(1)} %get-tuple-element.38.refs_2_, bf16[128,96,128]{2,1,0:T(8,128)(2,1)S(1)} %get-tuple-element.39.refs_3_, ...), custom_call_target="tpu_custom_call" | custom-call | flops 25165824 | tf_op jit(solution)/shard_map/gather_sums/pallas_call | solution.py:414
  50.1 2.8 %collective-permute-start.12 = (bf16[33,32,128]{2,1,0:T(8,128)(2,1)S(1)}, bf16[33,32,128]{2,1,0:T(8,128)(2,1)S(1)}, u32[]{:S(2)}, u32[]{:S(2)}) collective-permute-start(bf16[33,32,128]{2,1,0:T(8,128)(2,1)S(1)} %gather_sums.7), channel_id=1, source_target_pairs={{0,24},{1,25},{2,26},{3,27},{4,28},{5,29},{6,30},{7,31},{8,0},{9,1... | collective-permute-start | bytes 811016 | tf_op jit(solution)/shard_map/ppermute | solution.py:41
  52.9 2.6 %gather_sums.4.own_ref = f32[33,32,128]{2,1,0:T(8,128)S(1)} custom-call(bf16[512,384]{1,0:T(8,128)(2,1)S(1)} %get-tuple-element.51.refs_0_, bf16[128,96,128]{2,1,0:T(8,128)(2,1)S(1)} %get-tuple-element.37.refs_1_, bf16[128,96,128]{2,1,0:T(8,128)(2,1)S(1)} %get-tuple-element.38.refs_2_, bf16[128,96,128]{2,1,0:T(8,128)(2,1)S(1)} %get-tuple-element.39.refs_3_, ...), custom_call_target="tpu_custom_call" | custom-call | flops 25165824 | tf_op jit(solution)/shard_map/gather_sums/pallas_call | solution.py:414
  55.7 3.6 %collective-permute-done.11.refs_0_ = bf16[33,32,128]{2,1,0:T(8,128)(2,1)S(1)} collective-permute-done((bf16[33,32,128]{2,1,0:T(8,128)(2,1)S(1)}, bf16[33,32,128]{2,1,0:T(8,128)(2,1)S(1)}, u32[]{:S(2)}, u32[]{:S(2)}) %collective-permute-start.11) | collective-permute-done | bytes 270368 | tf_op jit(solution)/shard_map/ppermute | solution.py:41
  59.5 1.9 %collective-permute-start.13 = (bf16[9,32,128]{2,1,0:T(8,128)(2,1)S(1)}, bf16[9,32,128]{2,1,0:T(8,128)(2,1)S(1)}, u32[]{:S(2)}, u32[]{:S(2)}) collective-permute-start(bf16[9,32,128]{2,1,0:T(8,128)(2,1)S(1)} %get-tuple-element.54), channel_id=1, source_target_pairs={{0,1},{1,2},{2,3},{3,0},{4,5},{5,6},{6,7},{7,4},{8,9},{9,10},{10,1... | collective-permute-start | bytes 221192 | tf_op jit(solution)/shard_map/ppermute | solution.py:41
  61.4 1.8 %collective-permute-start.14 = (bf16[9,32,128]{2,1,0:T(8,128)(2,1)S(1)}, bf16[9,32,128]{2,1,0:T(8,128)(2,1)S(1)}, u32[]{:S(2)}, u32[]{:S(2)}) collective-permute-start(bf16[9,32,128]{2,1,0:T(8,128)(2,1)S(1)} %get-tuple-element.55), channel_id=1, source_target_pairs={{0,2},{1,3},{2,0},{3,1},{4,6},{5,7},{6,4},{7,5},{8,10},{9,11},{10,... | collective-permute-start | bytes 221192 | tf_op jit(solution)/shard_map/ppermute | solution.py:41
  65.0 2.2 %collective-permute-done.14.refs_1_ = bf16[9,32,128]{2,1,0:T(8,128)(2,1)S(1)} collective-permute-done((bf16[9,32,128]{2,1,0:T(8,128)(2,1)S(1)}, bf16[9,32,128]{2,1,0:T(8,128)(2,1)S(1)}, u32[]{:S(2)}, u32[]{:S(2)}) %collective-permute-start.14) | collective-permute-done | bytes 73760 | tf_op jit(solution)/shard_map/ppermute | solution.py:41
  67.7 2.7 %collective-permute-start.16 = (bf16[5,32,128]{2,1,0:T(8,128)(2,1)S(1)}, bf16[5,32,128]{2,1,0:T(8,128)(2,1)S(1)}, u32[]{:S(2)}, u32[]{:S(2)}) collective-permute-start(bf16[5,32,128]{2,1,0:T(8,128)(2,1)S(1)} %get-tuple-element.58), channel_id=1, source_target_pairs={{0,4},{1,5},{2,6},{3,7},{4,0},{5,1},{6,2},{7,3},{8,12},{9,13},{10,... | collective-permute-start | bytes 122888 | tf_op jit(solution)/shard_map/ppermute | solution.py:41
  71.0 2.2 %collective-permute-done.16.refs_0_ = bf16[5,32,128]{2,1,0:T(8,128)(2,1)S(1)} collective-permute-done((bf16[5,32,128]{2,1,0:T(8,128)(2,1)S(1)}, bf16[5,32,128]{2,1,0:T(8,128)(2,1)S(1)}, u32[]{:S(2)}, u32[]{:S(2)}) %collective-permute-start.16) | collective-permute-done | bytes 40992 | tf_op jit(solution)/shard_map/ppermute | solution.py:41
  (41 shorter events, 15.5 us)
Async XLA Ops:
  0.6 6.7 %collective-permute-start = (bf16[32,4,128]{2,1,0:T(4,128)(2,1)}, bf16[32,4,128]{2,1,0:T(4,128)(2,1)S(1)}, u32[]{:S(2)}, u32[]{:S(2)}) collective-permute-start(bf16[32,4,128]{2,1,0:T(4,128)(2,1)} %refs_0_.1), channel_id=1, source_target_pairs={{0,4},{1,5},{2,6},{3,7},{4,0},{5,1},{6,2},{7,3},{8,12},{9,13},{10,... | collective-permute-start | bytes 98312 | tf_op jit(solution)/shard_map/ppermute | solution.py:41
  4.7 0.7 copy-start.1
  5.4 2.0 %copy-start = (bf16[32,4,128]{2,1,0:T(4,128)(2,1)S(1)}, bf16[32,4,128]{2,1,0:T(4,128)(2,1)}, u32[]{:S(2)}) copy-start(bf16[32,4,128]{2,1,0:T(4,128)(2,1)} %refs_0_.1) | copy-start | bytes 98308
  7.5 9.1 %collective-permute-start.1 = (bf16[8,32,128]{2,1,0:T(8,128)(2,1)S(1)}, bf16[8,32,128]{2,1,0:T(8,128)(2,1)S(1)}, u32[]{:S(2)}, u32[]{:S(2)}) collective-permute-start(bf16[8,32,128]{2,1,0:T(8,128)(2,1)S(1)} %join.3.refs_0_), channel_id=1, source_target_pairs={{0,3},{1,0},{2,1},{3,2},{4,7},{5,4},{6,5},{7,6},{8,11},{9,8},{10,9... | collective-permute-start | bytes 196616 | tf_op jit(solution)/shard_map/ppermute | solution.py:41
  10.5 6.0 %collective-permute-start.2 = (bf16[8,32,128]{2,1,0:T(8,128)(2,1)S(1)}, bf16[8,32,128]{2,1,0:T(8,128)(2,1)S(1)}, u32[]{:S(2)}, u32[]{:S(2)}) collective-permute-start(bf16[8,32,128]{2,1,0:T(8,128)(2,1)S(1)} %join.3.refs_0_), channel_id=1, source_target_pairs={{0,2},{1,3},{2,0},{3,1},{4,6},{5,7},{6,4},{7,5},{8,10},{9,11},{10,... | collective-permute-start | bytes 196616 | tf_op jit(solution)/shard_map/ppermute | solution.py:41
  11.2 5.8 %collective-permute-start.3 = (bf16[8,32,128]{2,1,0:T(8,128)(2,1)S(1)}, bf16[8,32,128]{2,1,0:T(8,128)(2,1)S(1)}, u32[]{:S(2)}, u32[]{:S(2)}) collective-permute-start(bf16[8,32,128]{2,1,0:T(8,128)(2,1)S(1)} %join.3.refs_0_), channel_id=1, source_target_pairs={{0,1},{1,2},{2,3},{3,0},{4,5},{5,6},{6,7},{7,4},{8,9},{9,10},{10,1... | collective-permute-start | bytes 196616 | tf_op jit(solution)/shard_map/ppermute | solution.py:41
  17.0 11.3 %collective-permute-start.6 = (bf16[32,32,128]{2,1,0:T(8,128)(2,1)S(1)}, bf16[32,32,128]{2,1,0:T(8,128)(2,1)S(1)}, u32[]{:S(2)}, u32[]{:S(2)}) collective-permute-start(bf16[32,32,128]{2,1,0:T(8,128)(2,1)S(1)} %join.4.refs_0_), channel_id=1, source_target_pairs={{0,8},{1,9},{2,10},{3,11},{4,12},{5,13},{6,14},{7,15},{8,16},{9,17... | collective-permute-start | bytes 786440 | tf_op jit(solution)/shard_map/ppermute | solution.py:41
  18.6 12.8 %collective-permute-start.5 = (bf16[32,32,128]{2,1,0:T(8,128)(2,1)S(1)}, bf16[32,32,128]{2,1,0:T(8,128)(2,1)S(1)}, u32[]{:S(2)}, u32[]{:S(2)}) collective-permute-start(bf16[32,32,128]{2,1,0:T(8,128)(2,1)S(1)} %join.4.refs_0_), channel_id=1, source_target_pairs={{0,16},{1,17},{2,18},{3,19},{4,20},{5,21},{6,22},{7,23},{8,24},{9,... | collective-permute-start | bytes 786440 | tf_op jit(solution)/shard_map/ppermute | solution.py:41
  23.3 10.1 %collective-permute-start.4 = (bf16[32,32,128]{2,1,0:T(8,128)(2,1)S(1)}, bf16[32,32,128]{2,1,0:T(8,128)(2,1)S(1)}, u32[]{:S(2)}, u32[]{:S(2)}) collective-permute-start(bf16[32,32,128]{2,1,0:T(8,128)(2,1)S(1)} %join.5), channel_id=1, source_target_pairs={{0,24},{1,25},{2,26},{3,27},{4,28},{5,29},{6,30},{7,31},{8,0},{9,1... | collective-permute-start | bytes 786440 | tf_op jit(solution)/shard_map/ppermute | solution.py:41
  24.9 1.4 %copy-start.2 = (s32[384]{0:T(512)S(1)}, s32[384]{0:T(512)}, u32[]{:S(2)}) copy-start(s32[384]{0:T(512)} %param.11) | copy-start | bytes 4612
  35.9 2.2 %collective-permute-start.7 = (f32[16,384]{1,0:T(8,128)S(1)}, f32[16,384]{1,0:T(8,128)S(1)}, u32[]{:S(2)}, u32[]{:S(2)}) collective-permute-start(f32[16,384]{1,0:T(8,128)S(1)} %get-tuple-element.50.own_ref), channel_id=1, source_target_pairs={{0,32},{32,0},{64,96},{96,64},{1,33},{33,1},{65,97},{97,65},{2,34}... | collective-permute-start | bytes 73736 | tf_op jit(solution)/shard_map/ppermute | solution.py:511
  36.0 3.9 %collective-permute-start.8 = (f32[16,384]{1,0:T(8,128)S(1)}, f32[16,384]{1,0:T(8,128)S(1)}, u32[]{:S(2)}, u32[]{:S(2)}) collective-permute-start(f32[16,384]{1,0:T(8,128)S(1)} %get-tuple-element.50.own_ref), channel_id=1, source_target_pairs={{0,64},{32,96},{64,0},{96,32},{1,65},{33,97},{65,1},{97,33},{2,66}... | collective-permute-start | bytes 73736 | tf_op jit(solution)/shard_map/ppermute | solution.py:511
  37.1 3.3 %collective-permute-start.9 = (f32[16,384]{1,0:T(8,128)S(1)}, f32[16,384]{1,0:T(8,128)S(1)}, u32[]{:S(2)}, u32[]{:S(2)}) collective-permute-start(f32[16,384]{1,0:T(8,128)S(1)} %get-tuple-element.50.own_ref), channel_id=1, source_target_pairs={{0,96},{32,64},{64,32},{96,0},{1,97},{33,65},{65,33},{97,1},{2,98}... | collective-permute-start | bytes 73736 | tf_op jit(solution)/shard_map/ppermute | solution.py:511
  43.3 12.3 %collective-permute-start.10 = (bf16[33,32,128]{2,1,0:T(8,128)(2,1)S(1)}, bf16[33,32,128]{2,1,0:T(8,128)(2,1)S(1)}, u32[]{:S(2)}, u32[]{:S(2)}) collective-permute-start(bf16[33,32,128]{2,1,0:T(8,128)(2,1)S(1)} %gather_sums.5), channel_id=1, source_target_pairs={{0,16},{1,17},{2,18},{3,19},{4,20},{5,21},{6,22},{7,23},{8,24},{9,... | collective-permute-start | bytes 811016 | tf_op jit(solution)/shard_map/ppermute | solution.py:41
  46.9 12.3 %collective-permute-start.11 = (bf16[33,32,128]{2,1,0:T(8,128)(2,1)S(1)}, bf16[33,32,128]{2,1,0:T(8,128)(2,1)S(1)}, u32[]{:S(2)}, u32[]{:S(2)}) collective-permute-start(bf16[33,32,128]{2,1,0:T(8,128)(2,1)S(1)} %gather_sums.6), channel_id=1, source_target_pairs={{0,8},{1,9},{2,10},{3,11},{4,12},{5,13},{6,14},{7,15},{8,16},{9,17... | collective-permute-start | bytes 811016 | tf_op jit(solution)/shard_map/ppermute | solution.py:41
  50.1 9.2 %collective-permute-start.12 = (bf16[33,32,128]{2,1,0:T(8,128)(2,1)S(1)}, bf16[33,32,128]{2,1,0:T(8,128)(2,1)S(1)}, u32[]{:S(2)}, u32[]{:S(2)}) collective-permute-start(bf16[33,32,128]{2,1,0:T(8,128)(2,1)S(1)} %gather_sums.7), channel_id=1, source_target_pairs={{0,24},{1,25},{2,26},{3,27},{4,28},{5,29},{6,30},{7,31},{8,0},{9,1... | collective-permute-start | bytes 811016 | tf_op jit(solution)/shard_map/ppermute | solution.py:41
  59.5 5.6 %collective-permute-start.13 = (bf16[9,32,128]{2,1,0:T(8,128)(2,1)S(1)}, bf16[9,32,128]{2,1,0:T(8,128)(2,1)S(1)}, u32[]{:S(2)}, u32[]{:S(2)}) collective-permute-start(bf16[9,32,128]{2,1,0:T(8,128)(2,1)S(1)} %get-tuple-element.54), channel_id=1, source_target_pairs={{0,1},{1,2},{2,3},{3,0},{4,5},{5,6},{6,7},{7,4},{8,9},{9,10},{10,1... | collective-permute-start | bytes 221192 | tf_op jit(solution)/shard_map/ppermute | solution.py:41
  61.4 5.9 %collective-permute-start.14 = (bf16[9,32,128]{2,1,0:T(8,128)(2,1)S(1)}, bf16[9,32,128]{2,1,0:T(8,128)(2,1)S(1)}, u32[]{:S(2)}, u32[]{:S(2)}) collective-permute-start(bf16[9,32,128]{2,1,0:T(8,128)(2,1)S(1)} %get-tuple-element.55), channel_id=1, source_target_pairs={{0,2},{1,3},{2,0},{3,1},{4,6},{5,7},{6,4},{7,5},{8,10},{9,11},{10,... | collective-permute-start | bytes 221192 | tf_op jit(solution)/shard_map/ppermute | solution.py:41
  63.2 4.4 %collective-permute-start.15 = (bf16[9,32,128]{2,1,0:T(8,128)(2,1)S(1)}, bf16[9,32,128]{2,1,0:T(8,128)(2,1)S(1)}, u32[]{:S(2)}, u32[]{:S(2)}) collective-permute-start(bf16[9,32,128]{2,1,0:T(8,128)(2,1)S(1)} %get-tuple-element.56), channel_id=1, source_target_pairs={{0,3},{1,0},{2,1},{3,2},{4,7},{5,4},{6,5},{7,6},{8,11},{9,8},{10,9... | collective-permute-start | bytes 221192 | tf_op jit(solution)/shard_map/ppermute | solution.py:41
  67.7 5.5 %collective-permute-start.16 = (bf16[5,32,128]{2,1,0:T(8,128)(2,1)S(1)}, bf16[5,32,128]{2,1,0:T(8,128)(2,1)S(1)}, u32[]{:S(2)}, u32[]{:S(2)}) collective-permute-start(bf16[5,32,128]{2,1,0:T(8,128)(2,1)S(1)} %get-tuple-element.58), channel_id=1, source_target_pairs={{0,4},{1,5},{2,6},{3,7},{4,0},{5,1},{6,2},{7,3},{8,12},{9,13},{10,... | collective-permute-start | bytes 122888 | tf_op jit(solution)/shard_map/ppermute | solution.py:41

commit v4 on v3

--- a/solution.py
+++ b/solution.py
@@ -173,8 +173,9 @@
     def kernel(*refs):
         out_ref = refs[-1]
         for i, ref in enumerate(refs[: len(pieces)]):
+            block = ref[...].astype(F32) if turned else None
             for j in range(rows):
-                out_ref[i * rows + j] = ref[:, j, :] if turned else ref[j]
+                out_ref[i * rows + j] = block[:, j, :].astype(BF16) if turned else ref[j]
 
     return pl.pallas_call(
         kernel,

time: 74.4 us -> 74.3 us (level)
  no operation moved by 1% of the time
where the time goes in v4:
time: 74.3 us; the launch traced here: 74.1 us
  Pallas kernels  30.7 us (41%)
  starting transfers between devices  28.5 us (38%)
  waiting for transfers between devices  12.8 us (17%)
  local copies, waits for them, and re-layouts  1.29 us (2%)
  between operations  0.86 us (1%)
    ppermute x14, starting transfers between devices, send(): return lax.ppermute(value, 'dom', shift(dx, dz, dy))  26.5 us
    pallas_call x4, Pallas kernels, gather_sums(): pl.pallas_call(kernel, out_shape=jax.ShapeDtypeStruct((length + 1, classe...  10.6 us
    ppermute x14, waiting for transfers between devices, send(): return lax.ppermute(value, 'dom', shift(dx, dz, dy))  10.6 us
    pallas_call x4, Pallas kernels, weigh(): pl.pallas_call(kernel, out_shape=(pltpu.VMEM((cycles, rows, angles), BF16...  7.72 us
    pallas_call x3, Pallas kernels, correlate(): pl.pallas_call(kernel, out_shape=(pltpu.VMEM((count, wide), F32), pltpu.V...  5.87 us
    pallas_call x1, Pallas kernels, score(): pl.pallas_call(kernel, out_shape=(pltpu.VMEM((count, wide), F32), jax.Sha...  2.47 us
    ppermute x3, waiting for transfers between devices, local(): lax.ppermute(stats, 'cls', [(i, i ^ j) for i in range(4)])  2.22 us
    pallas_call x1, Pallas kernels, setup(): pl.pallas_call(setup_kernel, out_shape=(jax.ShapeDtypeStruct((count, cycl...  1.96 us
  transfers between devices with their start and end apart: 17, of which 9 were waited for; matrix products, arithmetic and copies ran while one was open for 1% of the time, Pallas kernels for 32%

profile of v4, /device:TPU:0, one launch (start us, length us, event | category | flops | bytes accessed | tf_op | source)
XLA Modules:
  0.0 74.1 jit_solution(3533549090446016298)
XLA Ops:
  0.6 4.0 %collective-permute-start = (bf16[32,4,128]{2,1,0:T(4,128)(2,1)}, bf16[32,4,128]{2,1,0:T(4,128)(2,1)S(1)}, u32[]{:S(2)}, u32[]{:S(2)}) collective-permute-start(bf16[32,4,128]{2,1,0:T(4,128)(2,1)} %refs_0_.1), channel_id=1, source_target_pairs={{0,4},{1,5},{2,6},{3,7},{4,0},{5,1},{6,2},{7,3},{8,12},{9,13},{10,... | collective-permute-start | bytes 98312 | tf_op jit(solution)/shard_map/ppermute | solution.py:41
  5.4 2.0 %setup.1 = (f32[384,128]{1,0:T(8,128)S(1)}, bf16[384,256]{1,0:T(8,128)(2,1)S(1)}, bf16[96,128,128]{2,1,0:T(8,128)(2,1)S(1)}) custom-call(s32[384]{0:T(512)S(1)} %copy-done.1, f32[64,128]{1,0:T(8,128)} %ctf_hbm.1, f32[1,128]{1,0:T(1,128)} %bitcast.1, bf16[384,128,128]{2,1,0:T(8,128)(2,1)} %particles_hbm.9), custom_call_target="tpu_custom_call" | custom-call | tf_op jit(solution)/shard_map/setup/pallas_call | solution.py:92
  7.4 3.1 %collective-permute-start.1 = (bf16[8,32,128]{2,1,0:T(8,128)(2,1)S(1)}, bf16[8,32,128]{2,1,0:T(8,128)(2,1)S(1)}, u32[]{:S(2)}, u32[]{:S(2)}) collective-permute-start(bf16[8,32,128]{2,1,0:T(8,128)(2,1)S(1)} %join.3.refs_0_), channel_id=1, source_target_pairs={{0,3},{1,0},{2,1},{3,2},{4,7},{5,4},{6,5},{7,6},{8,11},{9,8},{10,9... | collective-permute-start | bytes 196616 | tf_op jit(solution)/shard_map/ppermute | solution.py:41
  12.1 2.5 %weigh.4 = (bf16[128,96,128]{2,1,0:T(8,128)(2,1)S(1)}, f32[8,128]{1,0:T(8,128)}, bf16[96,128,128]{2,1,0:T(8,128)(2,1)S(1)}) custom-call(bf16[384,128,128]{2,1,0:T(8,128)(2,1)} %particles_hbm.9, bf16[96,128,128]{2,1,0:T(8,128)(2,1)S(1)} %get-tuple-element.32.here_ref, f32[384,128]{1,0:T(8,128)S(1)} %get-tuple-element.31.refs_2_.weight_ref), custom_call_target="tpu_custom_call" | custom-call | bytes 393216 | tf_op jit(solution)/shard_map/weigh/pallas_call | solution.py:154
  14.6 1.9 %weigh.5 = (bf16[128,96,128]{2,1,0:T(8,128)(2,1)S(1)}, f32[8,128]{1,0:T(8,128)S(1)}, bf16[96,128,128]{2,1,0:T(8,128)(2,1)S(1)}) custom-call(bf16[384,128,128]{2,1,0:T(8,128)(2,1)} %particles_hbm.9, bf16[96,128,128]{2,1,0:T(8,128)(2,1)S(1)} %get-tuple-element.33.here_ref, f32[384,128]{1,0:T(8,128)S(1)} %get-tuple-element.31.refs_2_.weight_ref), custom_call_target="tpu_custom_call" | custom-call | bytes 393216 | tf_op jit(solution)/shard_map/weigh/pallas_call | solution.py:154
  18.6 2.7 %collective-permute-start.5 = (bf16[32,32,128]{2,1,0:T(8,128)(2,1)S(1)}, bf16[32,32,128]{2,1,0:T(8,128)(2,1)S(1)}, u32[]{:S(2)}, u32[]{:S(2)}) collective-permute-start(bf16[32,32,128]{2,1,0:T(8,128)(2,1)S(1)} %join.4.refs_0_), channel_id=1, source_target_pairs={{0,16},{1,17},{2,18},{3,19},{4,20},{5,21},{6,22},{7,23},{8,24},{9,... | collective-permute-start | bytes 786440 | tf_op jit(solution)/shard_map/ppermute | solution.py:41
  21.3 1.9 %weigh.6 = (bf16[128,96,128]{2,1,0:T(8,128)(2,1)S(1)}, f32[8,128]{1,0:T(8,128)S(1)}, bf16[96,128,128]{2,1,0:T(8,128)(2,1)S(1)}) custom-call(bf16[384,128,128]{2,1,0:T(8,128)(2,1)} %particles_hbm.9, bf16[96,128,128]{2,1,0:T(8,128)(2,1)S(1)} %get-tuple-element.35.here_ref, f32[384,128]{1,0:T(8,128)S(1)} %get-tuple-element.31.refs_2_.weight_ref), custom_call_target="tpu_custom_call" | custom-call | bytes 393216 | tf_op jit(solution)/shard_map/weigh/pallas_call | solution.py:154
  23.2 1.7 %collective-permute-start.4 = (bf16[32,32,128]{2,1,0:T(8,128)(2,1)S(1)}, bf16[32,32,128]{2,1,0:T(8,128)(2,1)S(1)}, u32[]{:S(2)}, u32[]{:S(2)}) collective-permute-start(bf16[32,32,128]{2,1,0:T(8,128)(2,1)S(1)} %join.5), channel_id=1, source_target_pairs={{0,24},{1,25},{2,26},{3,27},{4,28},{5,29},{6,30},{7,31},{8,0},{9,1... | collective-permute-start | bytes 786440 | tf_op jit(solution)/shard_map/ppermute | solution.py:41
  26.4 2.0 %correlate.3 = (f32[384,512]{1,0:T(8,128)S(1)}, f32[32,128]{1,0:T(8,128)S(1)}) custom-call(bf16[32,32,128]{2,1,0:T(8,128)(2,1)S(1)} %join.4.refs_0_, bf16[128,96,128]{2,1,0:T(8,128)(2,1)S(1)} %get-tuple-element.37.refs_1_, bf16[128,96,128]{2,1,0:T(8,128)(2,1)S(1)} %get-tuple-element.38.refs_2_, bf16[128,96,128]{2,1,0:T(8,128)(2,1)S(1)} %get-tuple-element.39.refs_3_, ...), custom_call_target="tpu_custom_call" | custom-call | flops 25165824 | tf_op jit(solution)/shard_map/correlate/pallas_call | solution.py:245
  28.3 2.0 %correlate.4 = (f32[384,512]{1,0:T(8,128)S(1)}, f32[32,128]{1,0:T(8,128)S(1)}) custom-call(bf16[32,32,128]{2,1,0:T(8,128)(2,1)S(1)} %collective-permute-done.6.refs_0_, bf16[128,96,128]{2,1,0:T(8,128)(2,1)S(1)} %get-tuple-element.37.refs_1_, bf16[128,96,128]{2,1,0:T(8,128)(2,1)S(1)} %get-tuple-element.38.refs_2_, ...), custom_call_target="tpu_custom_call" | custom-call | flops 25165824 | tf_op jit(solution)/shard_map/correlate/pallas_call | solution.py:245
  31.4 2.0 %correlate.5 = (f32[384,512]{1,0:T(8,128)S(1)}, f32[32,128]{1,0:T(8,128)S(1)}) custom-call(bf16[32,32,128]{2,1,0:T(8,128)(2,1)S(1)} %collective-permute-done.5.refs_0_, bf16[128,96,128]{2,1,0:T(8,128)(2,1)S(1)} %get-tuple-element.37.refs_1_, bf16[128,96,128]{2,1,0:T(8,128)(2,1)S(1)} %get-tuple-element.38.refs_2_, ...), custom_call_target="tpu_custom_call" | custom-call | flops 25165824 | tf_op jit(solution)/shard_map/correlate/pallas_call | solution.py:245
  33.4 2.5 %score.1 = (f32[384,512]{1,0:T(8,128)S(1)}, f32[16,384]{1,0:T(8,128)S(1)}) custom-call(bf16[32,32,128]{2,1,0:T(8,128)(2,1)S(1)} %collective-permute-done.4.refs_0_, bf16[128,96,128]{2,1,0:T(8,128)(2,1)S(1)} %get-tuple-element.37.refs_1_, bf16[128,96,128]{2,1,0:T(8,128)(2,1)S(1)} %get-tuple-element.38.refs_2_, ...), custom_call_target="tpu_custom_call" | custom-call | flops 25165824 | tf_op jit(solution)/shard_map/score/pallas_call | solution.py:302
  38.1 1.8 %collective-permute-done.8.b_ref = f32[16,384]{1,0:T(8,128)S(1)} collective-permute-done((f32[16,384]{1,0:T(8,128)S(1)}, f32[16,384]{1,0:T(8,128)S(1)}, u32[]{:S(2)}, u32[]{:S(2)}) %collective-permute-start.8) | collective-permute-done | bytes 24608 | tf_op jit(solution)/shard_map/ppermute | solution.py:512
  40.6 2.7 %gather_sums.5 = bf16[33,32,128]{2,1,0:T(8,128)(2,1)S(1)} custom-call(bf16[512,384]{1,0:T(8,128)(2,1)S(1)} %get-tuple-element.51.refs_0_, bf16[128,96,128]{2,1,0:T(8,128)(2,1)S(1)} %get-tuple-element.37.refs_1_, bf16[128,96,128]{2,1,0:T(8,128)(2,1)S(1)} %get-tuple-element.38.refs_2_, bf16[128,96,128]{2,1,0:T(8,128)(2,1)S(1)} %get-tuple-element.39.refs_3_, ...), custom_call_target="tpu_custom_call" | custom-call | flops 25165824 | tf_op jit(solution)/shard_map/gather_sums/pallas_call | solution.py:415
  44.2 2.7 %gather_sums.6 = bf16[33,32,128]{2,1,0:T(8,128)(2,1)S(1)} custom-call(bf16[512,384]{1,0:T(8,128)(2,1)S(1)} %get-tuple-element.51.refs_0_, bf16[128,96,128]{2,1,0:T(8,128)(2,1)S(1)} %get-tuple-element.37.refs_1_, bf16[128,96,128]{2,1,0:T(8,128)(2,1)S(1)} %get-tuple-element.38.refs_2_, bf16[128,96,128]{2,1,0:T(8,128)(2,1)S(1)} %get-tuple-element.39.refs_3_, ...), custom_call_target="tpu_custom_call" | custom-call | flops 25165824 | tf_op jit(solution)/shard_map/gather_sums/pallas_call | solution.py:415
  47.4 2.7 %gather_sums.7 = bf16[33,32,128]{2,1,0:T(8,128)(2,1)S(1)} custom-call(bf16[512,384]{1,0:T(8,128)(2,1)S(1)} %get-tuple-element.51.refs_0_, bf16[128,96,128]{2,1,0:T(8,128)(2,1)S(1)} %get-tuple-element.37.refs_1_, bf16[128,96,128]{2,1,0:T(8,128)(2,1)S(1)} %get-tuple-element.38.refs_2_, bf16[128,96,128]{2,1,0:T(8,128)(2,1)S(1)} %get-tuple-element.39.refs_3_, ...), custom_call_target="tpu_custom_call" | custom-call | flops 25165824 | tf_op jit(solution)/shard_map/gather_sums/pallas_call | solution.py:415
  50.1 2.8 %collective-permute-start.12 = (bf16[33,32,128]{2,1,0:T(8,128)(2,1)S(1)}, bf16[33,32,128]{2,1,0:T(8,128)(2,1)S(1)}, u32[]{:S(2)}, u32[]{:S(2)}) collective-permute-start(bf16[33,32,128]{2,1,0:T(8,128)(2,1)S(1)} %gather_sums.7), channel_id=1, source_target_pairs={{0,24},{1,25},{2,26},{3,27},{4,28},{5,29},{6,30},{7,31},{8,0},{9,1... | collective-permute-start | bytes 811016 | tf_op jit(solution)/shard_map/ppermute | solution.py:41
  52.9 2.6 %gather_sums.4.own_ref = f32[33,32,128]{2,1,0:T(8,128)S(1)} custom-call(bf16[512,384]{1,0:T(8,128)(2,1)S(1)} %get-tuple-element.51.refs_0_, bf16[128,96,128]{2,1,0:T(8,128)(2,1)S(1)} %get-tuple-element.37.refs_1_, bf16[128,96,128]{2,1,0:T(8,128)(2,1)S(1)} %get-tuple-element.38.refs_2_, bf16[128,96,128]{2,1,0:T(8,128)(2,1)S(1)} %get-tuple-element.39.refs_3_, ...), custom_call_target="tpu_custom_call" | custom-call | flops 25165824 | tf_op jit(solution)/shard_map/gather_sums/pallas_call | solution.py:415
  55.6 3.6 %collective-permute-done.11.refs_0_ = bf16[33,32,128]{2,1,0:T(8,128)(2,1)S(1)} collective-permute-done((bf16[33,32,128]{2,1,0:T(8,128)(2,1)S(1)}, bf16[33,32,128]{2,1,0:T(8,128)(2,1)S(1)}, u32[]{:S(2)}, u32[]{:S(2)}) %collective-permute-start.11) | collective-permute-done | bytes 270368 | tf_op jit(solution)/shard_map/ppermute | solution.py:41
  59.4 1.9 %collective-permute-start.13 = (bf16[9,32,128]{2,1,0:T(8,128)(2,1)S(1)}, bf16[9,32,128]{2,1,0:T(8,128)(2,1)S(1)}, u32[]{:S(2)}, u32[]{:S(2)}) collective-permute-start(bf16[9,32,128]{2,1,0:T(8,128)(2,1)S(1)} %get-tuple-element.54), channel_id=1, source_target_pairs={{0,1},{1,2},{2,3},{3,0},{4,5},{5,6},{6,7},{7,4},{8,9},{9,10},{10,1... | collective-permute-start | bytes 221192 | tf_op jit(solution)/shard_map/ppermute | solution.py:41
  61.3 1.8 %collective-permute-start.14 = (bf16[9,32,128]{2,1,0:T(8,128)(2,1)S(1)}, bf16[9,32,128]{2,1,0:T(8,128)(2,1)S(1)}, u32[]{:S(2)}, u32[]{:S(2)}) collective-permute-start(bf16[9,32,128]{2,1,0:T(8,128)(2,1)S(1)} %get-tuple-element.55), channel_id=1, source_target_pairs={{0,2},{1,3},{2,0},{3,1},{4,6},{5,7},{6,4},{7,5},{8,10},{9,11},{10,... | collective-permute-start | bytes 221192 | tf_op jit(solution)/shard_map/ppermute | solution.py:41
  65.0 2.2 %collective-permute-done.14.refs_1_ = bf16[9,32,128]{2,1,0:T(8,128)(2,1)S(1)} collective-permute-done((bf16[9,32,128]{2,1,0:T(8,128)(2,1)S(1)}, bf16[9,32,128]{2,1,0:T(8,128)(2,1)S(1)}, u32[]{:S(2)}, u32[]{:S(2)}) %collective-permute-start.14) | collective-permute-done | bytes 73760 | tf_op jit(solution)/shard_map/ppermute | solution.py:41
  67.7 2.7 %collective-permute-start.16 = (bf16[5,32,128]{2,1,0:T(8,128)(2,1)S(1)}, bf16[5,32,128]{2,1,0:T(8,128)(2,1)S(1)}, u32[]{:S(2)}, u32[]{:S(2)}) collective-permute-start(bf16[5,32,128]{2,1,0:T(8,128)(2,1)S(1)} %get-tuple-element.58), channel_id=1, source_target_pairs={{0,4},{1,5},{2,6},{3,7},{4,0},{5,1},{6,2},{7,3},{8,12},{9,13},{10,... | collective-permute-start | bytes 122888 | tf_op jit(solution)/shard_map/ppermute | solution.py:41
  71.0 2.2 %collective-permute-done.16.refs_0_ = bf16[5,32,128]{2,1,0:T(8,128)(2,1)S(1)} collective-permute-done((bf16[5,32,128]{2,1,0:T(8,128)(2,1)S(1)}, bf16[5,32,128]{2,1,0:T(8,128)(2,1)S(1)}, u32[]{:S(2)}, u32[]{:S(2)}) %collective-permute-start.16) | collective-permute-done | bytes 40992 | tf_op jit(solution)/shard_map/ppermute | solution.py:41
  (41 shorter events, 15.5 us)
Async XLA Ops:
  0.6 6.7 %collective-permute-start = (bf16[32,4,128]{2,1,0:T(4,128)(2,1)}, bf16[32,4,128]{2,1,0:T(4,128)(2,1)S(1)}, u32[]{:S(2)}, u32[]{:S(2)}) collective-permute-start(bf16[32,4,128]{2,1,0:T(4,128)(2,1)} %refs_0_.1), channel_id=1, source_target_pairs={{0,4},{1,5},{2,6},{3,7},{4,0},{5,1},{6,2},{7,3},{8,12},{9,13},{10,... | collective-permute-start | bytes 98312 | tf_op jit(solution)/shard_map/ppermute | solution.py:41
  4.7 0.7 copy-start.1
  5.4 2.0 %copy-start = (bf16[32,4,128]{2,1,0:T(4,128)(2,1)S(1)}, bf16[32,4,128]{2,1,0:T(4,128)(2,1)}, u32[]{:S(2)}) copy-start(bf16[32,4,128]{2,1,0:T(4,128)(2,1)} %refs_0_.1) | copy-start | bytes 98308
  7.4 9.1 %collective-permute-start.1 = (bf16[8,32,128]{2,1,0:T(8,128)(2,1)S(1)}, bf16[8,32,128]{2,1,0:T(8,128)(2,1)S(1)}, u32[]{:S(2)}, u32[]{:S(2)}) collective-permute-start(bf16[8,32,128]{2,1,0:T(8,128)(2,1)S(1)} %join.3.refs_0_), channel_id=1, source_target_pairs={{0,3},{1,0},{2,1},{3,2},{4,7},{5,4},{6,5},{7,6},{8,11},{9,8},{10,9... | collective-permute-start | bytes 196616 | tf_op jit(solution)/shard_map/ppermute | solution.py:41
  10.5 6.0 %collective-permute-start.2 = (bf16[8,32,128]{2,1,0:T(8,128)(2,1)S(1)}, bf16[8,32,128]{2,1,0:T(8,128)(2,1)S(1)}, u32[]{:S(2)}, u32[]{:S(2)}) collective-permute-start(bf16[8,32,128]{2,1,0:T(8,128)(2,1)S(1)} %join.3.refs_0_), channel_id=1, source_target_pairs={{0,2},{1,3},{2,0},{3,1},{4,6},{5,7},{6,4},{7,5},{8,10},{9,11},{10,... | collective-permute-start | bytes 196616 | tf_op jit(solution)/shard_map/ppermute | solution.py:41
  11.1 5.8 %collective-permute-start.3 = (bf16[8,32,128]{2,1,0:T(8,128)(2,1)S(1)}, bf16[8,32,128]{2,1,0:T(8,128)(2,1)S(1)}, u32[]{:S(2)}, u32[]{:S(2)}) collective-permute-start(bf16[8,32,128]{2,1,0:T(8,128)(2,1)S(1)} %join.3.refs_0_), channel_id=1, source_target_pairs={{0,1},{1,2},{2,3},{3,0},{4,5},{5,6},{6,7},{7,4},{8,9},{9,10},{10,1... | collective-permute-start | bytes 196616 | tf_op jit(solution)/shard_map/ppermute | solution.py:41
  17.0 11.3 %collective-permute-start.6 = (bf16[32,32,128]{2,1,0:T(8,128)(2,1)S(1)}, bf16[32,32,128]{2,1,0:T(8,128)(2,1)S(1)}, u32[]{:S(2)}, u32[]{:S(2)}) collective-permute-start(bf16[32,32,128]{2,1,0:T(8,128)(2,1)S(1)} %join.4.refs_0_), channel_id=1, source_target_pairs={{0,8},{1,9},{2,10},{3,11},{4,12},{5,13},{6,14},{7,15},{8,16},{9,17... | collective-permute-start | bytes 786440 | tf_op jit(solution)/shard_map/ppermute | solution.py:41
  18.6 12.8 %collective-permute-start.5 = (bf16[32,32,128]{2,1,0:T(8,128)(2,1)S(1)}, bf16[32,32,128]{2,1,0:T(8,128)(2,1)S(1)}, u32[]{:S(2)}, u32[]{:S(2)}) collective-permute-start(bf16[32,32,128]{2,1,0:T(8,128)(2,1)S(1)} %join.4.refs_0_), channel_id=1, source_target_pairs={{0,16},{1,17},{2,18},{3,19},{4,20},{5,21},{6,22},{7,23},{8,24},{9,... | collective-permute-start | bytes 786440 | tf_op jit(solution)/shard_map/ppermute | solution.py:41
  23.2 10.1 %collective-permute-start.4 = (bf16[32,32,128]{2,1,0:T(8,128)(2,1)S(1)}, bf16[32,32,128]{2,1,0:T(8,128)(2,1)S(1)}, u32[]{:S(2)}, u32[]{:S(2)}) collective-permute-start(bf16[32,32,128]{2,1,0:T(8,128)(2,1)S(1)} %join.5), channel_id=1, source_target_pairs={{0,24},{1,25},{2,26},{3,27},{4,28},{5,29},{6,30},{7,31},{8,0},{9,1... | collective-permute-start | bytes 786440 | tf_op jit(solution)/shard_map/ppermute | solution.py:41
  24.9 1.4 %copy-start.2 = (s32[384]{0:T(512)S(1)}, s32[384]{0:T(512)}, u32[]{:S(2)}) copy-start(s32[384]{0:T(512)} %param.11) | copy-start | bytes 4612
  35.8 2.2 %collective-permute-start.7 = (f32[16,384]{1,0:T(8,128)S(1)}, f32[16,384]{1,0:T(8,128)S(1)}, u32[]{:S(2)}, u32[]{:S(2)}) collective-permute-start(f32[16,384]{1,0:T(8,128)S(1)} %get-tuple-element.50.own_ref), channel_id=1, source_target_pairs={{0,32},{32,0},{64,96},{96,64},{1,33},{33,1},{65,97},{97,65},{2,34}... | collective-permute-start | bytes 73736 | tf_op jit(solution)/shard_map/ppermute | solution.py:512
  35.9 3.9 %collective-permute-start.8 = (f32[16,384]{1,0:T(8,128)S(1)}, f32[16,384]{1,0:T(8,128)S(1)}, u32[]{:S(2)}, u32[]{:S(2)}) collective-permute-start(f32[16,384]{1,0:T(8,128)S(1)} %get-tuple-element.50.own_ref), channel_id=1, source_target_pairs={{0,64},{32,96},{64,0},{96,32},{1,65},{33,97},{65,1},{97,33},{2,66}... | collective-permute-start | bytes 73736 | tf_op jit(solution)/shard_map/ppermute | solution.py:512
  37.0 3.3 %collective-permute-start.9 = (f32[16,384]{1,0:T(8,128)S(1)}, f32[16,384]{1,0:T(8,128)S(1)}, u32[]{:S(2)}, u32[]{:S(2)}) collective-permute-start(f32[16,384]{1,0:T(8,128)S(1)} %get-tuple-element.50.own_ref), channel_id=1, source_target_pairs={{0,96},{32,64},{64,32},{96,0},{1,97},{33,65},{65,33},{97,1},{2,98}... | collective-permute-start | bytes 73736 | tf_op jit(solution)/shard_map/ppermute | solution.py:512
  43.3 12.3 %collective-permute-start.10 = (bf16[33,32,128]{2,1,0:T(8,128)(2,1)S(1)}, bf16[33,32,128]{2,1,0:T(8,128)(2,1)S(1)}, u32[]{:S(2)}, u32[]{:S(2)}) collective-permute-start(bf16[33,32,128]{2,1,0:T(8,128)(2,1)S(1)} %gather_sums.5), channel_id=1, source_target_pairs={{0,16},{1,17},{2,18},{3,19},{4,20},{5,21},{6,22},{7,23},{8,24},{9,... | collective-permute-start | bytes 811016 | tf_op jit(solution)/shard_map/ppermute | solution.py:41
  46.9 12.3 %collective-permute-start.11 = (bf16[33,32,128]{2,1,0:T(8,128)(2,1)S(1)}, bf16[33,32,128]{2,1,0:T(8,128)(2,1)S(1)}, u32[]{:S(2)}, u32[]{:S(2)}) collective-permute-start(bf16[33,32,128]{2,1,0:T(8,128)(2,1)S(1)} %gather_sums.6), channel_id=1, source_target_pairs={{0,8},{1,9},{2,10},{3,11},{4,12},{5,13},{6,14},{7,15},{8,16},{9,17... | collective-permute-start | bytes 811016 | tf_op jit(solution)/shard_map/ppermute | solution.py:41
  50.1 9.2 %collective-permute-start.12 = (bf16[33,32,128]{2,1,0:T(8,128)(2,1)S(1)}, bf16[33,32,128]{2,1,0:T(8,128)(2,1)S(1)}, u32[]{:S(2)}, u32[]{:S(2)}) collective-permute-start(bf16[33,32,128]{2,1,0:T(8,128)(2,1)S(1)} %gather_sums.7), channel_id=1, source_target_pairs={{0,24},{1,25},{2,26},{3,27},{4,28},{5,29},{6,30},{7,31},{8,0},{9,1... | collective-permute-start | bytes 811016 | tf_op jit(solution)/shard_map/ppermute | solution.py:41
  59.4 5.6 %collective-permute-start.13 = (bf16[9,32,128]{2,1,0:T(8,128)(2,1)S(1)}, bf16[9,32,128]{2,1,0:T(8,128)(2,1)S(1)}, u32[]{:S(2)}, u32[]{:S(2)}) collective-permute-start(bf16[9,32,128]{2,1,0:T(8,128)(2,1)S(1)} %get-tuple-element.54), channel_id=1, source_target_pairs={{0,1},{1,2},{2,3},{3,0},{4,5},{5,6},{6,7},{7,4},{8,9},{9,10},{10,1... | collective-permute-start | bytes 221192 | tf_op jit(solution)/shard_map/ppermute | solution.py:41
  61.3 5.9 %collective-permute-start.14 = (bf16[9,32,128]{2,1,0:T(8,128)(2,1)S(1)}, bf16[9,32,128]{2,1,0:T(8,128)(2,1)S(1)}, u32[]{:S(2)}, u32[]{:S(2)}) collective-permute-start(bf16[9,32,128]{2,1,0:T(8,128)(2,1)S(1)} %get-tuple-element.55), channel_id=1, source_target_pairs={{0,2},{1,3},{2,0},{3,1},{4,6},{5,7},{6,4},{7,5},{8,10},{9,11},{10,... | collective-permute-start | bytes 221192 | tf_op jit(solution)/shard_map/ppermute | solution.py:41
  63.2 4.4 %collective-permute-start.15 = (bf16[9,32,128]{2,1,0:T(8,128)(2,1)S(1)}, bf16[9,32,128]{2,1,0:T(8,128)(2,1)S(1)}, u32[]{:S(2)}, u32[]{:S(2)}) collective-permute-start(bf16[9,32,128]{2,1,0:T(8,128)(2,1)S(1)} %get-tuple-element.56), channel_id=1, source_target_pairs={{0,3},{1,0},{2,1},{3,2},{4,7},{5,4},{6,5},{7,6},{8,11},{9,8},{10,9... | collective-permute-start | bytes 221192 | tf_op jit(solution)/shard_map/ppermute | solution.py:41
  67.7 5.5 %collective-permute-start.16 = (bf16[5,32,128]{2,1,0:T(8,128)(2,1)S(1)}, bf16[5,32,128]{2,1,0:T(8,128)(2,1)S(1)}, u32[]{:S(2)}, u32[]{:S(2)}) collective-permute-start(bf16[5,32,128]{2,1,0:T(8,128)(2,1)S(1)} %get-tuple-element.58), channel_id=1, source_target_pairs={{0,4},{1,5},{2,6},{3,7},{4,0},{5,1},{6,2},{7,3},{8,12},{9,13},{10,... | collective-permute-start | bytes 122888 | tf_op jit(solution)/shard_map/ppermute | solution.py:41

commit v5 on v4

--- a/solution.py
+++ b/solution.py
@@ -501,12 +501,9 @@
         images.append(image)
         if part == 1:
             piece = join([piece] + from_y, token)
-        if part == 2:
-            late = join([piece], token)
-    blocks = [piece] + [send(late if d == 1 else piece, -d, 0, 0) for d in (1, 2, 3)]
-
-    before = correlate((0,), blocks[:1], images, None)
-    before = correlate((3,), [blocks[3]], images, before)
+    blocks = [piece] + [send(piece, -d, 0, 0) for d in (1, 2, 3)]
+
+    before = correlate((0, 3), [blocks[0], blocks[3]], images, None)
     before = correlate((2,), [blocks[2]], images, before)
     expo, stats = score((1,), [blocks[1]], images, before, power_pair, prior_rot)
     others = [lax.ppermute(stats, "cls", [(i, i ^ j) for i in range(4)]) for j in (1, 2, 3)]

time: 74.3 us -> 74.6 us (level)
  waiting for transfers between devices: 12.8 us -> 11.9 us
    ppermute x14, waiting for transfers between devices: 10.6 us -> 9.68 us  [send(): return lax.ppermute(value, 'dom', shift(dx, dz, dy))]
    pallas_call x3 -> x2, Pallas kernels: 5.87 us -> 5.54 us  [correlate(): pl.pallas_call(kernel, out_shape=(pltpu.VMEM((count, wide), F32), pltpu.V...]
  transfers between devices with their start and end apart: 17 -> 17, of which waited for: 9 -> 9; matrix products, arithmetic and copies ran while one was open for 1% -> 1% of each run, Pallas kernels for 32% -> 33%
where the time goes in v5:
time: 74.6 us; the launch traced here: 74.1 us
  Pallas kernels  31 us (42%)
  starting transfers between devices  29.1 us (39%)
  waiting for transfers between devices  11.9 us (16%)
  local copies, waits for them, and re-layouts  1.29 us (2%)
  between operations  0.85 us (1%)
    ppermute x14, starting transfers between devices, send(): return lax.ppermute(value, 'dom', shift(dx, dz, dy))  27.2 us
    pallas_call x4, Pallas kernels, gather_sums(): pl.pallas_call(kernel, out_shape=jax.ShapeDtypeStruct((length + 1, classe...  10.6 us
    ppermute x14, waiting for transfers between devices, send(): return lax.ppermute(value, 'dom', shift(dx, dz, dy))  9.68 us
    pallas_call x4, Pallas kernels, weigh(): pl.pallas_call(kernel, out_shape=(pltpu.VMEM((cycles, rows, angles), BF16...  8.31 us
    pallas_call x2, Pallas kernels, correlate(): pl.pallas_call(kernel, out_shape=(pltpu.VMEM((count, wide), F32), pltpu.V...  5.54 us
    pallas_call x1, Pallas kernels, score(): pl.pallas_call(kernel, out_shape=(pltpu.VMEM((count, wide), F32), jax.Sha...  2.47 us
    ppermute x3, waiting for transfers between devices, local(): lax.ppermute(stats, 'cls', [(i, i ^ j) for i in range(4)])  2.22 us
    pallas_call x1, Pallas kernels, setup(): pl.pallas_call(setup_kernel, out_shape=(jax.ShapeDtypeStruct((count, cycl...  1.96 us
  transfers between devices with their start and end apart: 17, of which 9 were waited for; matrix products, arithmetic and copies ran while one was open for 1% of the time, Pallas kernels for 33%

profile of v5, /device:TPU:0, one launch (start us, length us, event | category | flops | bytes accessed | tf_op | source)
XLA Modules:
  0.0 74.1 jit_solution(13511589407183277139)
XLA Ops:
  0.6 4.0 %collective-permute-start = (bf16[32,4,128]{2,1,0:T(4,128)(2,1)}, bf16[32,4,128]{2,1,0:T(4,128)(2,1)S(1)}, u32[]{:S(2)}, u32[]{:S(2)}) collective-permute-start(bf16[32,4,128]{2,1,0:T(4,128)(2,1)} %refs_0_.1), channel_id=1, source_target_pairs={{0,4},{1,5},{2,6},{3,7},{4,0},{5,1},{6,2},{7,3},{8,12},{9,13},{10,... | collective-permute-start | bytes 98312 | tf_op jit(solution)/shard_map/ppermute | solution.py:41
  5.4 2.0 %setup.1 = (f32[384,128]{1,0:T(8,128)S(1)}, bf16[384,256]{1,0:T(8,128)(2,1)S(1)}, bf16[96,128,128]{2,1,0:T(8,128)(2,1)S(1)}) custom-call(s32[384]{0:T(512)S(1)} %copy-done.1, f32[64,128]{1,0:T(8,128)} %ctf_hbm.1, f32[1,128]{1,0:T(1,128)} %bitcast.1, bf16[384,128,128]{2,1,0:T(8,128)(2,1)} %particles_hbm.9), custom_call_target="tpu_custom_call" | custom-call | tf_op jit(solution)/shard_map/setup/pallas_call | solution.py:92
  7.4 3.1 %collective-permute-start.1 = (bf16[8,32,128]{2,1,0:T(8,128)(2,1)S(1)}, bf16[8,32,128]{2,1,0:T(8,128)(2,1)S(1)}, u32[]{:S(2)}, u32[]{:S(2)}) collective-permute-start(bf16[8,32,128]{2,1,0:T(8,128)(2,1)S(1)} %join.2.refs_0_), channel_id=1, source_target_pairs={{0,3},{1,0},{2,1},{3,2},{4,7},{5,4},{6,5},{7,6},{8,11},{9,8},{10,9... | collective-permute-start | bytes 196616 | tf_op jit(solution)/shard_map/ppermute | solution.py:41
  12.1 2.5 %weigh.4 = (bf16[128,96,128]{2,1,0:T(8,128)(2,1)S(1)}, f32[8,128]{1,0:T(8,128)}, bf16[96,128,128]{2,1,0:T(8,128)(2,1)S(1)}) custom-call(bf16[384,128,128]{2,1,0:T(8,128)(2,1)} %particles_hbm.9, bf16[96,128,128]{2,1,0:T(8,128)(2,1)S(1)} %get-tuple-element.29.here_ref, f32[384,128]{1,0:T(8,128)S(1)} %get-tuple-element.28.refs_2_.weight_ref), custom_call_target="tpu_custom_call" | custom-call | bytes 393216 | tf_op jit(solution)/shard_map/weigh/pallas_call | solution.py:154
  14.6 1.9 %weigh.5 = (bf16[128,96,128]{2,1,0:T(8,128)(2,1)S(1)}, f32[8,128]{1,0:T(8,128)S(1)}, bf16[96,128,128]{2,1,0:T(8,128)(2,1)S(1)}) custom-call(bf16[384,128,128]{2,1,0:T(8,128)(2,1)} %particles_hbm.9, bf16[96,128,128]{2,1,0:T(8,128)(2,1)S(1)} %get-tuple-element.30.here_ref, f32[384,128]{1,0:T(8,128)S(1)} %get-tuple-element.28.refs_2_.weight_ref), custom_call_target="tpu_custom_call" | custom-call | bytes 393216 | tf_op jit(solution)/shard_map/weigh/pallas_call | solution.py:154
  17.0 1.6 %collective-permute-start.6 = (bf16[32,32,128]{2,1,0:T(8,128)(2,1)S(1)}, bf16[32,32,128]{2,1,0:T(8,128)(2,1)S(1)}, u32[]{:S(2)}, u32[]{:S(2)}) collective-permute-start(bf16[32,32,128]{2,1,0:T(8,128)(2,1)S(1)} %join.3.refs_0_), channel_id=1, source_target_pairs={{0,8},{1,9},{2,10},{3,11},{4,12},{5,13},{6,14},{7,15},{8,16},{9,17... | collective-permute-start | bytes 786440 | tf_op jit(solution)/shard_map/ppermute | solution.py:41
  18.6 2.7 %collective-permute-start.5 = (bf16[32,32,128]{2,1,0:T(8,128)(2,1)S(1)}, bf16[32,32,128]{2,1,0:T(8,128)(2,1)S(1)}, u32[]{:S(2)}, u32[]{:S(2)}) collective-permute-start(bf16[32,32,128]{2,1,0:T(8,128)(2,1)S(1)} %join.3.refs_0_), channel_id=1, source_target_pairs={{0,16},{1,17},{2,18},{3,19},{4,20},{5,21},{6,22},{7,23},{8,24},{9,... | collective-permute-start | bytes 786440 | tf_op jit(solution)/shard_map/ppermute | solution.py:41
  22.7 2.5 %weigh.6 = (bf16[128,96,128]{2,1,0:T(8,128)(2,1)S(1)}, f32[8,128]{1,0:T(8,128)}, bf16[96,128,128]{2,1,0:T(8,128)(2,1)S(1)}) custom-call(bf16[384,128,128]{2,1,0:T(8,128)(2,1)} %particles_hbm.9, bf16[96,128,128]{2,1,0:T(8,128)(2,1)S(1)} %get-tuple-element.34.here_ref, f32[384,128]{1,0:T(8,128)S(1)} %get-tuple-element.28.refs_2_.weight_ref), custom_call_target="tpu_custom_call" | custom-call | bytes 393216 | tf_op jit(solution)/shard_map/weigh/pallas_call | solution.py:154
  26.7 3.6 %correlate.2 = (f32[384,512]{1,0:T(8,128)S(1)}, f32[32,128]{1,0:T(8,128)S(1)}) custom-call(bf16[32,32,128]{2,1,0:T(8,128)(2,1)S(1)} %join.3.refs_0_, bf16[32,32,128]{2,1,0:T(8,128)(2,1)S(1)} %collective-permute-done.6.refs_1_, bf16[128,96,128]{2,1,0:T(8,128)(2,1)S(1)} %get-tuple-element.32.refs_2_.refs_1_, ...), custom_call_target="tpu_custom_call" | custom-call | flops 50331648 | tf_op jit(solution)/shard_map/correlate/pallas_call | solution.py:245
  31.4 2.0 %correlate.3 = (f32[384,512]{1,0:T(8,128)S(1)}, f32[32,128]{1,0:T(8,128)S(1)}) custom-call(bf16[32,32,128]{2,1,0:T(8,128)(2,1)S(1)} %collective-permute-done.5.refs_0_, bf16[128,96,128]{2,1,0:T(8,128)(2,1)S(1)} %get-tuple-element.32.refs_2_.refs_1_, bf16[128,96,128]{2,1,0:T(8,128)(2,1)S(1)} %get-tuple-element.33.refs_3_.refs_2_, ...), custom_call_target="tpu_custom_call" | custom-call | flops 25165824 | tf_op jit(solution)/shard_map/correlate/pallas_call | solution.py:245
  33.4 2.5 %score.1 = (f32[384,512]{1,0:T(8,128)S(1)}, f32[16,384]{1,0:T(8,128)S(1)}) custom-call(bf16[32,32,128]{2,1,0:T(8,128)(2,1)S(1)} %collective-permute-done.4.refs_0_, bf16[128,96,128]{2,1,0:T(8,128)(2,1)S(1)} %get-tuple-element.32.refs_2_.refs_1_, bf16[128,96,128]{2,1,0:T(8,128)(2,1)S(1)} %get-tuple-element.33.refs_3_.refs_2_, ...), custom_call_target="tpu_custom_call" | custom-call | flops 25165824 | tf_op jit(solution)/shard_map/score/pallas_call | solution.py:302
  38.1 1.8 %collective-permute-done.8.b_ref = f32[16,384]{1,0:T(8,128)S(1)} collective-permute-done((f32[16,384]{1,0:T(8,128)S(1)}, f32[16,384]{1,0:T(8,128)S(1)}, u32[]{:S(2)}, u32[]{:S(2)}) %collective-permute-start.8) | collective-permute-done | bytes 24608 | tf_op jit(solution)/shard_map/ppermute | solution.py:509
  40.6 2.7 %gather_sums.5 = bf16[33,32,128]{2,1,0:T(8,128)(2,1)S(1)} custom-call(bf16[512,384]{1,0:T(8,128)(2,1)S(1)} %get-tuple-element.45.refs_0_, bf16[128,96,128]{2,1,0:T(8,128)(2,1)S(1)} %get-tuple-element.32.refs_2_.refs_1_, bf16[128,96,128]{2,1,0:T(8,128)(2,1)S(1)} %get-tuple-element.33.refs_3_.refs_2_, ...), custom_call_target="tpu_custom_call" | custom-call | flops 25165824 | tf_op jit(solution)/shard_map/gather_sums/pallas_call | solution.py:415
  43.3 1.6 %collective-permute-start.10 = (bf16[33,32,128]{2,1,0:T(8,128)(2,1)S(1)}, bf16[33,32,128]{2,1,0:T(8,128)(2,1)S(1)}, u32[]{:S(2)}, u32[]{:S(2)}) collective-permute-start(bf16[33,32,128]{2,1,0:T(8,128)(2,1)S(1)} %gather_sums.5), channel_id=1, source_target_pairs={{0,16},{1,17},{2,18},{3,19},{4,20},{5,21},{6,22},{7,23},{8,24},{9,... | collective-permute-start | bytes 811016 | tf_op jit(solution)/shard_map/ppermute | solution.py:41
  44.9 2.7 %gather_sums.6 = bf16[33,32,128]{2,1,0:T(8,128)(2,1)S(1)} custom-call(bf16[512,384]{1,0:T(8,128)(2,1)S(1)} %get-tuple-element.45.refs_0_, bf16[128,96,128]{2,1,0:T(8,128)(2,1)S(1)} %get-tuple-element.32.refs_2_.refs_1_, bf16[128,96,128]{2,1,0:T(8,128)(2,1)S(1)} %get-tuple-element.33.refs_3_.refs_2_, ...), custom_call_target="tpu_custom_call" | custom-call | flops 25165824 | tf_op jit(solution)/shard_map/gather_sums/pallas_call | solution.py:415
  48.3 2.7 %gather_sums.7 = bf16[33,32,128]{2,1,0:T(8,128)(2,1)S(1)} custom-call(bf16[512,384]{1,0:T(8,128)(2,1)S(1)} %get-tuple-element.45.refs_0_, bf16[128,96,128]{2,1,0:T(8,128)(2,1)S(1)} %get-tuple-element.32.refs_2_.refs_1_, bf16[128,96,128]{2,1,0:T(8,128)(2,1)S(1)} %get-tuple-element.33.refs_3_.refs_2_, ...), custom_call_target="tpu_custom_call" | custom-call | flops 25165824 | tf_op jit(solution)/shard_map/gather_sums/pallas_call | solution.py:415
  50.9 2.7 %collective-permute-start.12 = (bf16[33,32,128]{2,1,0:T(8,128)(2,1)S(1)}, bf16[33,32,128]{2,1,0:T(8,128)(2,1)S(1)}, u32[]{:S(2)}, u32[]{:S(2)}) collective-permute-start(bf16[33,32,128]{2,1,0:T(8,128)(2,1)S(1)} %gather_sums.7), channel_id=1, source_target_pairs={{0,24},{1,25},{2,26},{3,27},{4,28},{5,29},{6,30},{7,31},{8,0},{9,1... | collective-permute-start | bytes 811016 | tf_op jit(solution)/shard_map/ppermute | solution.py:41
  53.6 2.6 %gather_sums.4.own_ref = f32[33,32,128]{2,1,0:T(8,128)S(1)} custom-call(bf16[512,384]{1,0:T(8,128)(2,1)S(1)} %get-tuple-element.45.refs_0_, bf16[128,96,128]{2,1,0:T(8,128)(2,1)S(1)} %get-tuple-element.32.refs_2_.refs_1_, bf16[128,96,128]{2,1,0:T(8,128)(2,1)S(1)} %get-tuple-element.33.refs_3_.refs_2_, ...), custom_call_target="tpu_custom_call" | custom-call | flops 25165824 | tf_op jit(solution)/shard_map/gather_sums/pallas_call | solution.py:415
  56.4 2.8 %collective-permute-done.11.refs_0_ = bf16[33,32,128]{2,1,0:T(8,128)(2,1)S(1)} collective-permute-done((bf16[33,32,128]{2,1,0:T(8,128)(2,1)S(1)}, bf16[33,32,128]{2,1,0:T(8,128)(2,1)S(1)}, u32[]{:S(2)}, u32[]{:S(2)}) %collective-permute-start.11) | collective-permute-done | bytes 270368 | tf_op jit(solution)/shard_map/ppermute | solution.py:41
  59.4 1.9 %collective-permute-start.13 = (bf16[9,32,128]{2,1,0:T(8,128)(2,1)S(1)}, bf16[9,32,128]{2,1,0:T(8,128)(2,1)S(1)}, u32[]{:S(2)}, u32[]{:S(2)}) collective-permute-start(bf16[9,32,128]{2,1,0:T(8,128)(2,1)S(1)} %get-tuple-element.48), channel_id=1, source_target_pairs={{0,1},{1,2},{2,3},{3,0},{4,5},{5,6},{6,7},{7,4},{8,9},{9,10},{10,1... | collective-permute-start | bytes 221192 | tf_op jit(solution)/shard_map/ppermute | solution.py:41
  61.3 1.8 %collective-permute-start.14 = (bf16[9,32,128]{2,1,0:T(8,128)(2,1)S(1)}, bf16[9,32,128]{2,1,0:T(8,128)(2,1)S(1)}, u32[]{:S(2)}, u32[]{:S(2)}) collective-permute-start(bf16[9,32,128]{2,1,0:T(8,128)(2,1)S(1)} %get-tuple-element.49), channel_id=1, source_target_pairs={{0,2},{1,3},{2,0},{3,1},{4,6},{5,7},{6,4},{7,5},{8,10},{9,11},{10,... | collective-permute-start | bytes 221192 | tf_op jit(solution)/shard_map/ppermute | solution.py:41
  65.0 2.2 %collective-permute-done.14.refs_1_ = bf16[9,32,128]{2,1,0:T(8,128)(2,1)S(1)} collective-permute-done((bf16[9,32,128]{2,1,0:T(8,128)(2,1)S(1)}, bf16[9,32,128]{2,1,0:T(8,128)(2,1)S(1)}, u32[]{:S(2)}, u32[]{:S(2)}) %collective-permute-start.14) | collective-permute-done | bytes 73760 | tf_op jit(solution)/shard_map/ppermute | solution.py:41
  67.7 2.9 %collective-permute-start.16 = (bf16[5,32,128]{2,1,0:T(8,128)(2,1)S(1)}, bf16[5,32,128]{2,1,0:T(8,128)(2,1)S(1)}, u32[]{:S(2)}, u32[]{:S(2)}) collective-permute-start(bf16[5,32,128]{2,1,0:T(8,128)(2,1)S(1)} %get-tuple-element.52), channel_id=1, source_target_pairs={{0,4},{1,5},{2,6},{3,7},{4,0},{5,1},{6,2},{7,3},{8,12},{9,13},{10,... | collective-permute-start | bytes 122888 | tf_op jit(solution)/shard_map/ppermute | solution.py:41
  71.1 2.1 %collective-permute-done.16.refs_0_ = bf16[5,32,128]{2,1,0:T(8,128)(2,1)S(1)} collective-permute-done((bf16[5,32,128]{2,1,0:T(8,128)(2,1)S(1)}, bf16[5,32,128]{2,1,0:T(8,128)(2,1)S(1)}, u32[]{:S(2)}, u32[]{:S(2)}) %collective-permute-start.16) | collective-permute-done | bytes 40992 | tf_op jit(solution)/shard_map/ppermute | solution.py:41
  (39 shorter events, 14.5 us)
Async XLA Ops:
  0.6 6.7 %collective-permute-start = (bf16[32,4,128]{2,1,0:T(4,128)(2,1)}, bf16[32,4,128]{2,1,0:T(4,128)(2,1)S(1)}, u32[]{:S(2)}, u32[]{:S(2)}) collective-permute-start(bf16[32,4,128]{2,1,0:T(4,128)(2,1)} %refs_0_.1), channel_id=1, source_target_pairs={{0,4},{1,5},{2,6},{3,7},{4,0},{5,1},{6,2},{7,3},{8,12},{9,13},{10,... | collective-permute-start | bytes 98312 | tf_op jit(solution)/shard_map/ppermute | solution.py:41
  4.7 0.7 copy-start.1
  5.4 2.0 %copy-start = (bf16[32,4,128]{2,1,0:T(4,128)(2,1)S(1)}, bf16[32,4,128]{2,1,0:T(4,128)(2,1)}, u32[]{:S(2)}) copy-start(bf16[32,4,128]{2,1,0:T(4,128)(2,1)} %refs_0_.1) | copy-start | bytes 98308
  7.4 9.1 %collective-permute-start.1 = (bf16[8,32,128]{2,1,0:T(8,128)(2,1)S(1)}, bf16[8,32,128]{2,1,0:T(8,128)(2,1)S(1)}, u32[]{:S(2)}, u32[]{:S(2)}) collective-permute-start(bf16[8,32,128]{2,1,0:T(8,128)(2,1)S(1)} %join.2.refs_0_), channel_id=1, source_target_pairs={{0,3},{1,0},{2,1},{3,2},{4,7},{5,4},{6,5},{7,6},{8,11},{9,8},{10,9... | collective-permute-start | bytes 196616 | tf_op jit(solution)/shard_map/ppermute | solution.py:41
  10.5 6.0 %collective-permute-start.2 = (bf16[8,32,128]{2,1,0:T(8,128)(2,1)S(1)}, bf16[8,32,128]{2,1,0:T(8,128)(2,1)S(1)}, u32[]{:S(2)}, u32[]{:S(2)}) collective-permute-start(bf16[8,32,128]{2,1,0:T(8,128)(2,1)S(1)} %join.2.refs_0_), channel_id=1, source_target_pairs={{0,2},{1,3},{2,0},{3,1},{4,6},{5,7},{6,4},{7,5},{8,10},{9,11},{10,... | collective-permute-start | bytes 196616 | tf_op jit(solution)/shard_map/ppermute | solution.py:41
  11.1 5.8 %collective-permute-start.3 = (bf16[8,32,128]{2,1,0:T(8,128)(2,1)S(1)}, bf16[8,32,128]{2,1,0:T(8,128)(2,1)S(1)}, u32[]{:S(2)}, u32[]{:S(2)}) collective-permute-start(bf16[8,32,128]{2,1,0:T(8,128)(2,1)S(1)} %join.2.refs_0_), channel_id=1, source_target_pairs={{0,1},{1,2},{2,3},{3,0},{4,5},{5,6},{6,7},{7,4},{8,9},{9,10},{10,1... | collective-permute-start | bytes 196616 | tf_op jit(solution)/shard_map/ppermute | solution.py:41
  17.0 9.7 %collective-permute-start.6 = (bf16[32,32,128]{2,1,0:T(8,128)(2,1)S(1)}, bf16[32,32,128]{2,1,0:T(8,128)(2,1)S(1)}, u32[]{:S(2)}, u32[]{:S(2)}) collective-permute-start(bf16[32,32,128]{2,1,0:T(8,128)(2,1)S(1)} %join.3.refs_0_), channel_id=1, source_target_pairs={{0,8},{1,9},{2,10},{3,11},{4,12},{5,13},{6,14},{7,15},{8,16},{9,17... | collective-permute-start | bytes 786440 | tf_op jit(solution)/shard_map/ppermute | solution.py:41
  18.6 12.8 %collective-permute-start.5 = (bf16[32,32,128]{2,1,0:T(8,128)(2,1)S(1)}, bf16[32,32,128]{2,1,0:T(8,128)(2,1)S(1)}, u32[]{:S(2)}, u32[]{:S(2)}) collective-permute-start(bf16[32,32,128]{2,1,0:T(8,128)(2,1)S(1)} %join.3.refs_0_), channel_id=1, source_target_pairs={{0,16},{1,17},{2,18},{3,19},{4,20},{5,21},{6,22},{7,23},{8,24},{9,... | collective-permute-start | bytes 786440 | tf_op jit(solution)/shard_map/ppermute | solution.py:41
  21.3 12.1 %collective-permute-start.4 = (bf16[32,32,128]{2,1,0:T(8,128)(2,1)S(1)}, bf16[32,32,128]{2,1,0:T(8,128)(2,1)S(1)}, u32[]{:S(2)}, u32[]{:S(2)}) collective-permute-start(bf16[32,32,128]{2,1,0:T(8,128)(2,1)S(1)} %join.3.refs_0_), channel_id=1, source_target_pairs={{0,24},{1,25},{2,26},{3,27},{4,28},{5,29},{6,30},{7,31},{8,0},{9,1... | collective-permute-start | bytes 786440 | tf_op jit(solution)/shard_map/ppermute | solution.py:41
  25.2 1.4 %copy-start.2 = (s32[384]{0:T(512)S(1)}, s32[384]{0:T(512)}, u32[]{:S(2)}) copy-start(s32[384]{0:T(512)} %param.11) | copy-start | bytes 4612
  35.8 2.2 %collective-permute-start.7 = (f32[16,384]{1,0:T(8,128)S(1)}, f32[16,384]{1,0:T(8,128)S(1)}, u32[]{:S(2)}, u32[]{:S(2)}) collective-permute-start(f32[16,384]{1,0:T(8,128)S(1)} %get-tuple-element.44.own_ref), channel_id=1, source_target_pairs={{0,32},{32,0},{64,96},{96,64},{1,33},{33,1},{65,97},{97,65},{2,34}... | collective-permute-start | bytes 73736 | tf_op jit(solution)/shard_map/ppermute | solution.py:509
  35.9 3.9 %collective-permute-start.8 = (f32[16,384]{1,0:T(8,128)S(1)}, f32[16,384]{1,0:T(8,128)S(1)}, u32[]{:S(2)}, u32[]{:S(2)}) collective-permute-start(f32[16,384]{1,0:T(8,128)S(1)} %get-tuple-element.44.own_ref), channel_id=1, source_target_pairs={{0,64},{32,96},{64,0},{96,32},{1,65},{33,97},{65,1},{97,33},{2,66}... | collective-permute-start | bytes 73736 | tf_op jit(solution)/shard_map/ppermute | solution.py:509
  37.0 3.3 %collective-permute-start.9 = (f32[16,384]{1,0:T(8,128)S(1)}, f32[16,384]{1,0:T(8,128)S(1)}, u32[]{:S(2)}, u32[]{:S(2)}) collective-permute-start(f32[16,384]{1,0:T(8,128)S(1)} %get-tuple-element.44.own_ref), channel_id=1, source_target_pairs={{0,96},{32,64},{64,32},{96,0},{1,97},{33,65},{65,33},{97,1},{2,98}... | collective-permute-start | bytes 73736 | tf_op jit(solution)/shard_map/ppermute | solution.py:509
  43.3 13.0 %collective-permute-start.10 = (bf16[33,32,128]{2,1,0:T(8,128)(2,1)S(1)}, bf16[33,32,128]{2,1,0:T(8,128)(2,1)S(1)}, u32[]{:S(2)}, u32[]{:S(2)}) collective-permute-start(bf16[33,32,128]{2,1,0:T(8,128)(2,1)S(1)} %gather_sums.5), channel_id=1, source_target_pairs={{0,16},{1,17},{2,18},{3,19},{4,20},{5,21},{6,22},{7,23},{8,24},{9,... | collective-permute-start | bytes 811016 | tf_op jit(solution)/shard_map/ppermute | solution.py:41
  47.6 11.6 %collective-permute-start.11 = (bf16[33,32,128]{2,1,0:T(8,128)(2,1)S(1)}, bf16[33,32,128]{2,1,0:T(8,128)(2,1)S(1)}, u32[]{:S(2)}, u32[]{:S(2)}) collective-permute-start(bf16[33,32,128]{2,1,0:T(8,128)(2,1)S(1)} %gather_sums.6), channel_id=1, source_target_pairs={{0,8},{1,9},{2,10},{3,11},{4,12},{5,13},{6,14},{7,15},{8,16},{9,17... | collective-permute-start | bytes 811016 | tf_op jit(solution)/shard_map/ppermute | solution.py:41
  50.9 8.4 %collective-permute-start.12 = (bf16[33,32,128]{2,1,0:T(8,128)(2,1)S(1)}, bf16[33,32,128]{2,1,0:T(8,128)(2,1)S(1)}, u32[]{:S(2)}, u32[]{:S(2)}) collective-permute-start(bf16[33,32,128]{2,1,0:T(8,128)(2,1)S(1)} %gather_sums.7), channel_id=1, source_target_pairs={{0,24},{1,25},{2,26},{3,27},{4,28},{5,29},{6,30},{7,31},{8,0},{9,1... | collective-permute-start | bytes 811016 | tf_op jit(solution)/shard_map/ppermute | solution.py:41
  59.4 5.6 %collective-permute-start.13 = (bf16[9,32,128]{2,1,0:T(8,128)(2,1)S(1)}, bf16[9,32,128]{2,1,0:T(8,128)(2,1)S(1)}, u32[]{:S(2)}, u32[]{:S(2)}) collective-permute-start(bf16[9,32,128]{2,1,0:T(8,128)(2,1)S(1)} %get-tuple-element.48), channel_id=1, source_target_pairs={{0,1},{1,2},{2,3},{3,0},{4,5},{5,6},{6,7},{7,4},{8,9},{9,10},{10,1... | collective-permute-start | bytes 221192 | tf_op jit(solution)/shard_map/ppermute | solution.py:41
  61.3 5.9 %collective-permute-start.14 = (bf16[9,32,128]{2,1,0:T(8,128)(2,1)S(1)}, bf16[9,32,128]{2,1,0:T(8,128)(2,1)S(1)}, u32[]{:S(2)}, u32[]{:S(2)}) collective-permute-start(bf16[9,32,128]{2,1,0:T(8,128)(2,1)S(1)} %get-tuple-element.49), channel_id=1, source_target_pairs={{0,2},{1,3},{2,0},{3,1},{4,6},{5,7},{6,4},{7,5},{8,10},{9,11},{10,... | collective-permute-start | bytes 221192 | tf_op jit(solution)/shard_map/ppermute | solution.py:41
  63.2 4.4 %collective-permute-start.15 = (bf16[9,32,128]{2,1,0:T(8,128)(2,1)S(1)}, bf16[9,32,128]{2,1,0:T(8,128)(2,1)S(1)}, u32[]{:S(2)}, u32[]{:S(2)}) collective-permute-start(bf16[9,32,128]{2,1,0:T(8,128)(2,1)S(1)} %get-tuple-element.50), channel_id=1, source_target_pairs={{0,3},{1,0},{2,1},{3,2},{4,7},{5,4},{6,5},{7,6},{8,11},{9,8},{10,9... | collective-permute-start | bytes 221192 | tf_op jit(solution)/shard_map/ppermute | solution.py:41
  67.7 5.5 %collective-permute-start.16 = (bf16[5,32,128]{2,1,0:T(8,128)(2,1)S(1)}, bf16[5,32,128]{2,1,0:T(8,128)(2,1)S(1)}, u32[]{:S(2)}, u32[]{:S(2)}) collective-permute-start(bf16[5,32,128]{2,1,0:T(8,128)(2,1)S(1)} %get-tuple-element.52), channel_id=1, source_target_pairs={{0,4},{1,5},{2,6},{3,7},{4,0},{5,1},{6,2},{7,3},{8,12},{9,13},{10,... | collective-permute-start | bytes 122888 | tf_op jit(solution)/shard_map/ppermute | solution.py:41
